TPU v7x, 256 devices: a whole 4x4x8 slice. The times are simulated.
256 devices in a mesh: dp: 32 (over y, z), mp: 8 (over x, core).
Axes of the slice: x: 4, y: 4, z: 8, core: 2. Of those that a mesh axis runs over, the one named last changes fastest.
Arguments:
- gradient: bfloat16 [32, 256, 28672], P('dp', None, 'mp'), may hold values from -6 to 6
- feedback: float32 [32, 256, 28672], P('dp', None, 'mp'), may hold values from -3 to 3
- warm_basis: float32 [32, 28672], P(None, 'mp'), may hold values from -6 to 6
Outputs:
- approx: bfloat16 [256, 28672], P(None, 'mp')
- new_feedback: float32 [32, 256, 28672], P('dp', None, 'mp')
All inputs are finite; a program needn't handle non-finite values.
Results may differ from a plain program's by a relative error of at most 0.001.
Values sent between devices are 32-bit elements; how exact they have to be, the bound alone decides.
No kernel may reach another device: no remote copies, remote signals or barrier semaphores. Data moves between devices by JAX's collectives and lax.ppermute only.
A program may use at most 64 MiB of HBM per device.

v0:
```python
import jax
import jax.numpy as jnp
from jax import lax
from jax.sharding import PartitionSpec as P


def lower_solve(factor_low, right_side):
    return jax.scipy.linalg.solve_triangular(factor_low, right_side, lower=True)


def rebuild(columns, factor, ortho_basis, replicas):
    approx = lax.dot_general(
        ortho_basis, factor, (((0,), (0,)), ((), ())), precision=lax.Precision.HIGHEST
    )
    return (approx, columns - approx / replicas)


def local(gradient, feedback, warm_basis):
    merged = gradient[0].astype(jnp.float32) + feedback[0]
    partial_value = lax.dot_general(
        warm_basis, merged, (((1,), (1,)), ((), ())), precision=lax.Precision.HIGHEST
    )
    summed = lax.psum(partial_value, ("dp", "mp"))
    gram_sum = jnp.dot(summed, summed.T, precision=lax.Precision.HIGHEST)
    factor_low = jnp.linalg.cholesky(gram_sum)
    ortho_basis = lower_solve(factor_low, summed)
    replicas = lax.axis_size("dp")
    factor = lax.psum(jnp.dot(ortho_basis, merged, precision=lax.Precision.HIGHEST), "dp")
    approx, updated = rebuild(merged, factor, ortho_basis, replicas)
    return (approx.astype(jnp.bfloat16), updated[None])


def solution(mesh):
    return jax.shard_map(
        local,
        mesh=mesh,
        in_specs=(P("dp", None, "mp"), P("dp", None, "mp"), P(None, "mp")),
        out_specs=(P(None, "mp"), P("dp", None, "mp")),
        check_vma=False,
    )
```

profile of v0, /device:TPU:2, one launch (start us, length us, event | category | flops | bytes accessed | tf_op | source)
XLA Modules:
  0.0 263.4 jit_solution(17443916665738353878)
XLA Ops:
  7.2 0.0 copy-start
  7.2 0.0 copy-start.1
  7.2 0.0 all-reduce.2.cloned.1.call-start
  7.2 1.0 copy-done
  8.2 5.8 %fusion.5 = f32[32,256]{1,0:T(8,128)S(1)} fusion(f32[32,3584]{1,0:T(8,128)S(1)} %copy-done, f32[1,256,3584]{2,1,0:T(8,128)} %param.4, bf16[1,256,3584]{2,1,0:T(8,128)(2,1)} %param.3), kind=kOutput, calls=%fused_computation.7 | convolution fusion | flops 354156544 | bytes 5996544 | tf_op jit(solution)/shard_map/dot_general | solution.py:20
  14.0 78.9 %psum.14 = f32[32,256]{1,0:T(8,128)S(1)} all-reduce(f32[32,256]{1,0:T(8,128)S(1)} %fusion.5), channel_id=1, replica_groups=mesh['dp'=32,'mp'=8] {'dp','mp'}, use_global_device_ids=true, to_apply=%region_0.0 | all-reduce | flops 8192 | bytes 65536 | tf_op jit(solution)/shard_map/psum | solution.py:23
  92.9 0.2 fusion.12
  93.1 0.1 copy.5
  93.1 2.9 %cholesky.16 = f32[32,32]{1,0:T(8,128)S(1)} custom-call(f32[32,32]{1,0:T(8,128)S(1)} %fusion.11), custom_call_target="Cholesky" | custom-call | tf_op jit(solution)/shard_map/jit(cholesky)/cholesky | solution.py:25
  96.1 0.6 compare_reduce_fusion
  96.7 0.7 fusion.8
  97.4 2.4 custom-call.7
  99.8 0.2 fusion.9
  100.1 0.0 copy-done.1
  100.1 5.2 %fusion = f32[32,3584]{1,0:T(8,128)} fusion(f32[32,256]{1,0:T(8,128)S(1)} %fusion.9, f32[1,256,3584]{2,1,0:T(8,128)} %param.4, bf16[1,256,3584]{2,1,0:T(8,128)(2,1)S(1)} %copy-done.1), kind=kOutput, calls=%fused_computation.1 | convolution fusion | flops 354156544 | bytes 5996544 | tf_op jit(solution)/shard_map/dot_general | solution.py:28
  105.3 0.0 all-reduce.2.cloned.1.call-update
  105.3 144.4 %all-reduce.2.cloned.1.call-done = f32[32,3584]{1,0:T(8,128)} async-done(((f32[32,3584]{1,0:T(8,128)}), f32[32,3584]{1,0:T(8,128)}) %all-reduce.2.cloned.1.call-update) | async-done | bytes 458768 | tf_op jit(solution)/shard_map/psum | solution.py:28
  249.8 6.8 %fusion.4 = (f32[1,256,3584]{2,1,0:T(8,128)}, bf16[256,3584]{1,0:T(8,128)(2,1)}) fusion(f32[1,256,3584]{2,1,0:T(8,128)} %param.4, bf16[1,256,3584]{2,1,0:T(8,128)(2,1)S(1)} %copy-done.1, f32[32,256]{1,0:T(8,128)S(1)} %fusion.9, f32[32,3584]{1,0:T(8,128)} %all-reduce.2.cloned.1.call-done), kind=kOutput, calls=%fused_computation.5 | convolution fusion | flops 356909056 | bytes 11501568 | tf_op jit(solution)/shard_map/dot_general | solution.py:12
  (2 shorter events, 0.0 us)
Async XLA Ops:
  7.2 1.0 copy-start
  7.2 92.9 %copy-start.1 = (bf16[1,256,3584]{2,1,0:T(8,128)(2,1)S(1)}, bf16[1,256,3584]{2,1,0:T(8,128)(2,1)}, u32[]{:S(2)}) copy-start(bf16[1,256,3584]{2,1,0:T(8,128)(2,1)} %param.3) | copy-start | bytes 5505028
  7.2 242.6 %all-reduce.2.cloned.1.call-start = ((), (), s32[]{:S(2)}) async-start(), calls=%async_computation | async-start | bytes 917504 | tf_op jit(solution)/shard_map/psum | solution.py:28
Sparse Core Ops, SparseCore 0:
  105.4 144.2 all-reduce.1
where the time goes:
time: 264 us; the launch traced here: 263 us
  waiting for transfers between devices  144 us (55%)
  blocking collectives  78.9 us (30%)
  matrix products  18.2 us (7%)
  between operations  14.1 us (5%)
  other arithmetic  6.69 us (3%)
    psum x1, waiting for transfers between devices, local(): lax.psum(jnp.dot(ortho_basis, merged, precision=lax.Precision.HIGHEST), '...  144 us
    psum x1, blocking collectives, local(): summed = lax.psum(partial_value, ('dp', 'mp'))  78.9 us
    dot_general x1, matrix products, rebuild(): lax.dot_general(ortho_basis, factor, (((0,), (0,)), ((), ())), precision=...  6.8 us
    dot_general x1, matrix products, local(): lax.dot_general(warm_basis, merged, (((1,), (1,)), ((), ())), precision=l...  5.81 us
  transfers between devices with their start and end apart: 1, of which 1 were waited for; matrix products, arithmetic and copies ran while one was open for 0% of the time, Pallas kernels for 0%

commit v1 on v0

v1 whole, which is shorter than its diff:
```python
import functools

import jax
import jax.numpy as jnp
from jax import lax
from jax.experimental import pallas as pl
from jax.experimental.pallas import tpu as pltpu
from jax.sharding import Mesh
from jax.sharding import PartitionSpec as P

VMEM_LIMIT = 24 * 1024 * 1024
F32 = jnp.float32
BF16 = jnp.bfloat16


def halves(value):
    high = value.astype(BF16)
    return high, (value - high.astype(F32)).astype(BF16)


def dot(a, b, ca, cb):
    return lax.dot_general(a, b, (((ca,), (cb,)), ((), ())), preferred_element_type=F32)


def project_kernel(gradient_ref, feedback_ref, basis_ref, merged_ref, projected_ref):
    merged = gradient_ref[...].astype(F32) + feedback_ref[...]
    merged_ref[...] = merged
    high, low = halves(merged)
    basis_high, basis_low = halves(basis_ref[...])
    rank = basis_high.shape[0]
    both = dot(jnp.concatenate([basis_high, basis_low], axis=0), high, 1, 1)
    term = both[:rank] + both[rank:] + dot(basis_high, low, 1, 1)

    @pl.when(pl.program_id(0) == 0)
    def _():
        projected_ref[...] = term

    @pl.when(pl.program_id(0) != 0)
    def _():
        projected_ref[...] += term


def project(gradient, feedback, basis, block):
    rows, cols = feedback.shape
    rank = basis.shape[0]
    return pl.pallas_call(
        project_kernel,
        grid=(cols // block,),
        in_specs=[
            pl.BlockSpec((rows, block), lambda i: (0, i)),
            pl.BlockSpec((rows, block), lambda i: (0, i)),
            pl.BlockSpec((rank, block), lambda i: (0, i)),
        ],
        out_specs=[
            pl.BlockSpec((rows, block), lambda i: (0, i)),
            pl.BlockSpec((rank, rows), lambda i: (0, 0)),
        ],
        out_shape=[
            jax.ShapeDtypeStruct((rows, cols), F32),
            jax.ShapeDtypeStruct((rank, rows), F32),
        ],
        compiler_params=pltpu.CompilerParams(vmem_limit_bytes=VMEM_LIMIT),
        name="project",
    )(gradient, feedback, basis)


def factor_kernel(projected_ref, merged_ref, *out_refs):
    high, low = halves(merged_ref[...])
    p_high, p_low = halves(projected_ref[...])
    rank = p_high.shape[0]
    both = dot(jnp.concatenate([p_high, p_low], axis=0), high, 1, 0)
    term = both[:rank] + both[rank:] + dot(p_high, low, 1, 0)
    depth = rank // len(out_refs)
    for k, out_ref in enumerate(out_refs):
        out_ref[...] = term[k * depth : (k + 1) * depth]


def partial_factor(projected, merged, pieces, block):
    rank, rows = projected.shape
    cols = merged.shape[1]
    depth = rank // pieces
    return pl.pallas_call(
        factor_kernel,
        grid=(cols // block,),
        in_specs=[
            pl.BlockSpec((rank, rows), lambda i: (0, 0)),
            pl.BlockSpec((rows, block), lambda i: (0, i)),
        ],
        out_specs=[pl.BlockSpec((depth, block), lambda i: (0, i))] * pieces,
        out_shape=[jax.ShapeDtypeStruct((depth, cols), F32)] * pieces,
        compiler_params=pltpu.CompilerParams(vmem_limit_bytes=VMEM_LIMIT),
        name="partial_factor",
    )(projected, merged)


def solve_kernel(projected_ref, out_ref):
    p = projected_ref[...]
    rank = p.shape[0]
    exact = functools.partial(
        lax.dot_general, precision=lax.Precision.HIGHEST, preferred_element_type=F32
    )
    gram = exact(p, p, (((1,), (1,)), ((), ())))
    eye = (
        lax.broadcasted_iota(jnp.int32, (rank, rank), 0)
        == lax.broadcasted_iota(jnp.int32, (rank, rank), 1)
    ).astype(F32)
    state = jnp.concatenate([gram, eye], axis=1)
    row_id = lax.broadcasted_iota(jnp.int32, (rank, 1), 0)
    inverse_pivots = jnp.zeros((rank, 1), F32)
    for k in range(rank):
        row = state[k : k + 1, :]
        inverse = 1.0 / state[k : k + 1, k : k + 1]
        inverse_pivots = jnp.where(row_id == k, inverse, inverse_pivots)
        if k + 1 < rank:
            multiplier = jnp.where(row_id > k, state[:, k : k + 1] * inverse, 0.0)
            state = state - multiplier * row
    unit = state[:, rank:]
    basis = exact(unit, p, (((1,), (0,)), ((), ()))) * inverse_pivots
    out_ref[...] = exact(unit, basis, (((0,), (0,)), ((), ())))


def solve(projected):
    return pl.pallas_call(
        solve_kernel,
        out_shape=jax.ShapeDtypeStruct(projected.shape, F32),
        name="solve",
    )(projected)


def rebuild_kernel(scale, basis_ref, merged_ref, *refs):
    *factor_refs, approx_ref, updated_ref = refs
    b_high, b_low = halves(basis_ref[...])
    f_high, f_low = halves(jnp.concatenate([r[...] for r in factor_refs], axis=0))
    left = jnp.concatenate([b_high, b_high, b_low], axis=0)
    right = jnp.concatenate([f_high, f_low, f_high], axis=0)
    approx = dot(left, right, 0, 0)
    approx_ref[...] = approx.astype(BF16)
    updated_ref[...] = merged_ref[...] - approx * scale


def rebuild(basis, merged, factors, replicas, block):
    rank, rows = basis.shape
    cols = merged.shape[1]
    depth = factors[0].shape[0]
    return pl.pallas_call(
        functools.partial(rebuild_kernel, 1.0 / replicas),
        grid=(cols // block,),
        in_specs=[
            pl.BlockSpec((rank, rows), lambda i: (0, 0)),
            pl.BlockSpec((rows, block), lambda i: (0, i)),
        ]
        + [pl.BlockSpec((depth, block), lambda i: (0, i))] * len(factors),
        out_specs=[pl.BlockSpec((rows, block), lambda i: (0, i))] * 2,
        out_shape=[
            jax.ShapeDtypeStruct((rows, cols), BF16),
            jax.ShapeDtypeStruct((rows, cols), F32),
        ],
        compiler_params=pltpu.CompilerParams(vmem_limit_bytes=VMEM_LIMIT),
        name="rebuild",
    )(basis, merged, *factors)


def rotate(x, axis, size, step):
    return lax.ppermute(x, axis, [(i, (i + step) % size) for i in range(size)])


def sum_over(x, axes, size):
    spread = jnp.broadcast_to(x[None], (size,) + x.shape)
    return jnp.sum(lax.all_to_all(spread, axes, 0, 0), axis=0)


def sum_everywhere(x, sizes):
    core = lax.axis_index("core")
    half = x.shape[0] // 2
    pair = x.reshape(2, half, x.shape[1])
    mine = lax.dynamic_index_in_dim(pair, core, 0, False)
    other = lax.dynamic_index_in_dim(pair, 1 - core, 0, False)
    mine = mine + rotate(other, "core", 2, 1)
    mine = sum_over(mine, ("y", "x"), sizes["y"] * sizes["x"])
    mine = sum_over(mine, "z", sizes["z"])
    other = rotate(mine, "core", 2, 1)
    return jnp.where(
        core == 0, jnp.concatenate([mine, other]), jnp.concatenate([other, mine])
    )


def local(sizes, gradient, feedback, warm_basis):
    y, z = sizes["y"], sizes["z"]
    merged, projected = project(gradient[0], feedback[0], warm_basis, 896)
    projected = sum_everywhere(projected, sizes)
    rank = projected.shape[0]
    depth = rank // y
    place = lax.axis_index("y")
    blocks = projected.reshape(y, depth, -1)
    ahead = jnp.concatenate(
        [lax.dynamic_index_in_dim(blocks, (place + k) % y, 0, False) for k in range(y)]
    )
    pieces = partial_factor(ahead, merged, y, 896)
    arrived = [rotate(pieces[k], "y", y, k) for k in range(1, y)]
    basis = solve(projected).reshape(y, depth, -1)
    mine = pieces[0] + sum(arrived[1:], arrived[0])
    cols = mine.shape[1]
    summed = jnp.sum(
        lax.all_to_all(mine.reshape(z, depth // z, cols), "z", 0, 0), axis=0
    )
    spread = jnp.broadcast_to(summed[None], (z,) + summed.shape)
    whole = lax.all_to_all(spread, "z", 0, 0).reshape(depth, cols)
    factors = [whole] + [rotate(whole, "y", y, k) for k in range(1, y)]
    behind = jnp.concatenate(
        [lax.dynamic_index_in_dim(basis, (place - k) % y, 0, False) for k in range(y)]
    )
    approx, updated = rebuild(behind, merged, factors, y * z, 896)
    return (approx, updated[None])


def solution(mesh):
    sizes = {"y": 4, "z": 8, "x": 4, "core": 2}
    inner = Mesh(mesh.devices.reshape(tuple(sizes.values())), tuple(sizes))
    dp, mp = ("y", "z"), ("x", "core")
    return jax.shard_map(
        functools.partial(local, sizes),
        mesh=inner,
        in_specs=(P(dp, None, mp), P(dp, None, mp), P(None, mp)),
        out_specs=(P(None, mp), P(dp, None, mp)),
        check_vma=False,
    )
```

time: 264 us -> 102 us (0.39)
  waiting for transfers between devices: 144 us -> 14.5 us
  blocking collectives: 78.9 us -> 54.8 us
  matrix products: 18.2 us -> 0 us
  between operations: 14.1 us -> 0.88 us
  Pallas kernels: 0 us -> 11.8 us
  local copies, waits for them, and re-layouts: 1.04 us -> 11.5 us
  starting transfers between devices: 0.04 us -> 7.02 us
  other arithmetic: 6.69 us -> 0.78 us
    psum x1 -> x0, waiting for transfers between devices: 144 us -> none  [local(): lax.psum(jnp.dot(ortho_basis, merged, precision=lax.Precision.HIGHEST), '...]
    psum x1 -> x0, blocking collectives: 78.9 us -> none  [local(): summed = lax.psum(partial_value, ('dp', 'mp'))]
    all_to_all x0 -> x4, blocking collectives: none -> 54.8 us  [the longest x2 32.3 us: sum_over(): return jnp.sum(lax.all_to_all(spread, axes, 0, 0), axis=0)]
    dot_general x4 -> x0, matrix products: 18 us -> none  [the longest x1 6.8 us: rebuild(): lax.dot_general(ortho_basis, factor, (((0,), (0,)), ((), ())), precision=...]
    ppermute x0 -> x8, waiting for transfers between devices: none -> 14.5 us  [rotate(): return lax.ppermute(x, axis, [(i, (i + step) % size) for i in range(size)])]
    pallas_call x0 -> x4, Pallas kernels: none -> 11.8 us  [the longest x1 4.74 us: solve(): pl.pallas_call(solve_kernel, out_shape=jax.ShapeDtypeStruct(projected.sha...]
    unnamed x4 -> x13, local copies, waits for them, and re-layouts: 0.96 us -> 10.5 us
    ppermute x0 -> x8, starting transfers between devices: none -> 7.02 us  [rotate(): return lax.ppermute(x, axis, [(i, (i + step) % size) for i in range(size)])]
  transfers between devices with their start and end apart: 1 -> 8, of which waited for: 1 -> 7; matrix products, arithmetic and copies ran while one was open for 0% -> 0% of each run, Pallas kernels for 0% -> 0%
where the time goes in v1:
time: 102 us; the launch traced here: 101 us
  blocking collectives  54.8 us (54%)
  waiting for transfers between devices  14.5 us (14%)
  Pallas kernels  11.8 us (12%)
  local copies, waits for them, and re-layouts  11.5 us (11%)
  starting transfers between devices  7.02 us (7%)
    all_to_all x2, blocking collectives, sum_over(): return jnp.sum(lax.all_to_all(spread, axes, 0, 0), axis=0)  32.3 us
    ppermute x8, waiting for transfers between devices, rotate(): return lax.ppermute(x, axis, [(i, (i + step) % size) for i in range(size)])  14.5 us
    all_to_all x1, blocking collectives, local(): lax.all_to_all(mine.reshape(z, depth // z, cols), 'z', 0, 0)  11.3 us
    all_to_all x1, blocking collectives, local(): whole = lax.all_to_all(spread, 'z', 0, 0).reshape(depth, cols)  11.3 us
    unnamed x13, local copies, waits for them, and re-layouts  10.5 us
    ppermute x8, starting transfers between devices, rotate(): return lax.ppermute(x, axis, [(i, (i + step) % size) for i in range(size)])  7.02 us
    pallas_call x1, Pallas kernels, solve(): pl.pallas_call(solve_kernel, out_shape=jax.ShapeDtypeStruct(projected.sha...  4.74 us
    pallas_call x1, Pallas kernels, rebuild(): pl.pallas_call(functools.partial(rebuild_kernel, 1.0 / replicas), grid=(c...  3.43 us
  transfers between devices with their start and end apart: 8, of which 7 were waited for; matrix products, arithmetic and copies ran while one was open for 0% of the time, Pallas kernels for 0%

profile of v1, /device:TPU:2, one launch (start us, length us, event | category | flops | bytes accessed | tf_op | source)
XLA Modules:
  0.0 101.3 jit_solution(10852327413906769018)
XLA Ops:
  0.6 0.0 copy-start.3
  0.6 2.0 %copy-done.3 = f32[1,256,3584]{2,1,0:T(8,128)S(1)} copy-done((f32[1,256,3584]{2,1,0:T(8,128)S(1)}, f32[1,256,3584]{2,1,0:T(8,128)}, u32[]{:S(2)}) %copy-start.3) | copy-done | bytes 3670040
  2.7 0.0 copy-start.4
  2.7 1.5 %copy-done.4 = bf16[1,256,3584]{2,1,0:T(8,128)(2,1)S(1)} copy-done((bf16[1,256,3584]{2,1,0:T(8,128)(2,1)S(1)}, bf16[1,256,3584]{2,1,0:T(8,128)(2,1)}, u32[]{:S(2)}) %copy-start.4) | copy-done | bytes 1835032
  4.2 0.0 copy-start.5
  4.2 1.0 %copy-done.5 = f32[32,3584]{1,0:T(8,128)S(1)} copy-done((f32[32,3584]{1,0:T(8,128)S(1)}, f32[32,3584]{1,0:T(8,128)}, u32[]{:S(2)}) %copy-start.5) | copy-done | bytes 458776
  5.2 2.3 %project.1 = (f32[256,3584]{1,0:T(8,128)S(1)}, f32[32,256]{1,0:T(8,128)S(1)}) custom-call(bf16[256,3584]{1,0:T(8,128)(2,1)S(1)} %bitcast.32, f32[256,3584]{1,0:T(8,128)S(1)} %bitcast.31, f32[32,3584]{1,0:T(8,128)S(1)} %copy-done.5), custom_call_target="tpu_custom_call" | custom-call | tf_op jit(solution)/shard_map/project/pallas_call | solution.py:46
  7.5 0.0 copy-start
  7.5 1.8 %copy-done = f32[256,3584]{1,0:T(8,128)} copy-done((f32[256,3584]{1,0:T(8,128)}, f32[256,3584]{1,0:T(8,128)S(1)}, u32[]{:S(2)}) %copy-start) | copy-done | bytes 3670040
  9.3 0.0 collective-permute-start
  9.3 1.2 %collective-permute-done = f32[16,256]{1,0:T(8,128)S(1)} collective-permute-done((f32[16,256]{1,0:T(8,128)S(1)}, f32[16,256]{1,0:T(8,128)S(1)}, u32[]{:S(2)}, u32[]{:S(2)}) %collective-permute-start) | collective-permute-done | bytes 16416 | tf_op jit(solution)/shard_map/ppermute | solution.py:164
  10.6 14.9 %all_to_all.20 = f32[16,16,256]{2,1,0:T(8,128)S(1)} all-to-all(f32[16,16,256]{2,1,0:T(8,128)S(1)} %broadcast_in_dim.8), channel_id=1, replica_groups=mesh['y'=4,'z'=8,'x'=4,'core'=2] {'y','x'}, dimensions={0} | all-to-all | bytes 524288 | tf_op jit(solution)/shard_map/all_to_all | solution.py:169
  25.5 17.3 %all_to_all.21 = f32[8,16,256]{2,1,0:T(8,128)S(1)} all-to-all(f32[8,16,256]{2,1,0:T(8,128)S(1)} %broadcast_in_dim.9), channel_id=1, replica_groups=mesh['y'=4,'z'=8,'x'=4,'core'=2] {'z'}, dimensions={0} | all-to-all | bytes 262144 | tf_op jit(solution)/shard_map/all_to_all | solution.py:169
  42.9 0.1 collective-permute-start.1
  43.1 1.0 %collective-permute-done.1 = f32[16,256]{1,0:T(8,128)S(1)} collective-permute-done((f32[16,256]{1,0:T(8,128)S(1)}, f32[16,256]{1,0:T(8,128)S(1)}, u32[]{:S(2)}, u32[]{:S(2)}) %collective-permute-start.1) | collective-permute-done | bytes 16416 | tf_op jit(solution)/shard_map/ppermute | solution.py:164
  44.1 0.6 maximum_select_fusion.projected_ref
  44.8 4.7 %solve.1 = f32[32,256]{1,0:T(8,128)} custom-call(f32[32,256]{1,0:T(8,128)} %maximum_select_fusion.projected_ref), custom_call_target="tpu_custom_call" | custom-call | tf_op jit(solution)/shard_map/solve/pallas_call | solution.py:123
  49.5 0.8 dynamic-slice_bitcast_fusion.4
  50.3 0.0 copy-start.1
  50.3 2.0 %copy-done.1 = f32[256,3584]{1,0:T(8,128)S(1)} copy-done((f32[256,3584]{1,0:T(8,128)S(1)}, f32[256,3584]{1,0:T(8,128)}, u32[]{:S(2)}) %copy-start.1) | copy-done | bytes 3670040
  52.4 1.4 %partial_factor.1 = (f32[8,3584]{1,0:T(8,128)S(1)}, f32[8,3584]{1,0:T(8,128)S(1)}, f32[8,3584]{1,0:T(8,128)S(1)}, f32[8,3584]{1,0:T(8,128)S(1)}) custom-call(f32[32,256]{1,0:T(8,128)S(1)} %pad_maximum_fusion.1.projected_ref, f32[256,3584]{1,0:T(8,128)S(1)} %copy-done.1), custom_call_target="tpu_custom_call" | custom-call | tf_op jit(solution)/shard_map/partial_factor/pallas_call | solution.py:82
  53.7 0.1 collective-permute-start.2
  53.8 2.3 %collective-permute-start.3 = (f32[8,3584]{1,0:T(8,128)S(1)}, f32[8,3584]{1,0:T(8,128)S(1)}, u32[]{:S(2)}, u32[]{:S(2)}) collective-permute-start(f32[8,3584]{1,0:T(8,128)S(1)} %get-tuple-element.14), channel_id=1, source_target_pairs={{0,128},{64,192},{128,0},{192,64},{1,129},{65,193},{129,1},{193,65... | collective-permute-start | bytes 344072 | tf_op jit(solution)/shard_map/ppermute | solution.py:164
  56.1 1.2 %collective-permute-start.4 = (f32[8,3584]{1,0:T(8,128)S(1)}, f32[8,3584]{1,0:T(8,128)S(1)}, u32[]{:S(2)}, u32[]{:S(2)}) collective-permute-start(f32[8,3584]{1,0:T(8,128)S(1)} %get-tuple-element.15), channel_id=1, source_target_pairs={{0,192},{64,0},{128,64},{192,128},{1,193},{65,1},{129,65},{193,129... | collective-permute-start | bytes 344072 | tf_op jit(solution)/shard_map/ppermute | solution.py:164
  57.3 5.4 %collective-permute-done.2 = f32[8,3584]{1,0:T(8,128)S(1)} collective-permute-done((f32[8,3584]{1,0:T(8,128)S(1)}, f32[8,3584]{1,0:T(8,128)S(1)}, u32[]{:S(2)}, u32[]{:S(2)}) %collective-permute-start.2) | collective-permute-done | bytes 114720 | tf_op jit(solution)/shard_map/ppermute | solution.py:164
  62.7 0.0 collective-permute-done.3
  62.7 0.6 collective-permute-done.4
  63.3 0.1 copy.6
  63.5 11.3 %all_to_all.22 = f32[8,1,3584]{2,1,0:T(1,128)S(1)} all-to-all(f32[8,1,3584]{2,1,0:T(1,128)S(1)} %copy.6), channel_id=1, replica_groups=mesh['y'=4,'z'=8,'x'=4,'core'=2] {'z'}, dimensions={0} | all-to-all | bytes 229376 | tf_op jit(solution)/shard_map/all_to_all | solution.py:204
  74.8 0.1 reduce_sum.29
  74.9 0.1 broadcast_in_dim.10
  74.9 11.3 %all_to_all.23 = f32[8,1,3584]{2,1,0:T(1,128)S(1)} all-to-all(f32[8,1,3584]{2,1,0:T(1,128)S(1)} %broadcast_in_dim.10), channel_id=1, replica_groups=mesh['y'=4,'z'=8,'x'=4,'core'=2] {'z'}, dimensions={0} | all-to-all | bytes 229376 | tf_op jit(solution)/shard_map/all_to_all | solution.py:207
  86.2 2.4 %collective-permute-start.7 = (f32[8,3584]{1,0:T(8,128)S(1)}, f32[8,3584]{1,0:T(8,128)S(1)}, u32[]{:S(2)}, u32[]{:S(2)}) collective-permute-start(f32[8,3584]{1,0:T(8,128)S(1)} %bitcast.33), channel_id=1, source_target_pairs={{0,192},{64,0},{128,64},{192,128},{1,193},{65,1},{129,65},{193,129... | collective-permute-start | bytes 344072 | tf_op jit(solution)/shard_map/ppermute | solution.py:164
  88.6 0.0 collective-permute-start.6
  88.6 1.0 collective-permute-start.5
  89.6 2.6 %collective-permute-done.7.refs_3_ = f32[8,3584]{1,0:T(8,128)S(1)} collective-permute-done((f32[8,3584]{1,0:T(8,128)S(1)}, f32[8,3584]{1,0:T(8,128)S(1)}, u32[]{:S(2)}, u32[]{:S(2)}) %collective-permute-start.7) | collective-permute-done | bytes 114720 | tf_op jit(solution)/shard_map/ppermute | solution.py:164
  92.2 2.8 %collective-permute-done.6.refs_2_ = f32[8,3584]{1,0:T(8,128)S(1)} collective-permute-done((f32[8,3584]{1,0:T(8,128)S(1)}, f32[8,3584]{1,0:T(8,128)S(1)}, u32[]{:S(2)}, u32[]{:S(2)}) %collective-permute-start.6) | collective-permute-done | bytes 114720 | tf_op jit(solution)/shard_map/ppermute | solution.py:164
  95.0 0.8 collective-permute-done.5.refs_1_
  95.9 0.0 copy-start.2
  95.9 2.0 %copy-done.2 = f32[256,3584]{1,0:T(8,128)S(1)} copy-done((f32[256,3584]{1,0:T(8,128)S(1)}, f32[256,3584]{1,0:T(8,128)}, u32[]{:S(2)}) %copy-start.2) | copy-done | bytes 3670040
  97.9 3.4 %rebuild.1 = (bf16[256,3584]{1,0:T(8,128)(2,1)}, f32[256,3584]{1,0:T(8,128)}) custom-call(f32[32,256]{1,0:T(8,128)S(1)} %pad_maximum_fusion.basis_ref, f32[256,3584]{1,0:T(8,128)S(1)} %copy-done.2, f32[8,3584]{1,0:T(8,128)S(1)} %bitcast.36, f32[8,3584]{1,0:T(8,128)S(1)} %collective-permute-done.5.refs_1_, f32[8,3584]{1,0:T(8,128)S(1)} %collective-permute-done.6.refs_2_, ...), custom_call_target="tpu_custom_call" | custom-call | tf_op jit(solution)/shard_map/rebuild/pallas_call | solution.py:145
  (10 shorter events, 0.1 us)
Async XLA Ops:
  0.6 2.0 %copy-start.3 = (f32[1,256,3584]{2,1,0:T(8,128)S(1)}, f32[1,256,3584]{2,1,0:T(8,128)}, u32[]{:S(2)}) copy-start(f32[1,256,3584]{2,1,0:T(8,128)} %param.4) | copy-start | bytes 11010052
  2.7 1.5 %copy-start.4 = (bf16[1,256,3584]{2,1,0:T(8,128)(2,1)S(1)}, bf16[1,256,3584]{2,1,0:T(8,128)(2,1)}, u32[]{:S(2)}) copy-start(bf16[1,256,3584]{2,1,0:T(8,128)(2,1)} %param.3) | copy-start | bytes 5505028
  4.2 1.0 %copy-start.5 = (f32[32,3584]{1,0:T(8,128)S(1)}, f32[32,3584]{1,0:T(8,128)}, u32[]{:S(2)}) copy-start(f32[32,3584]{1,0:T(8,128)} %basis_ref.1) | copy-start | bytes 1376260
  7.5 1.8 %copy-start = (f32[256,3584]{1,0:T(8,128)}, f32[256,3584]{1,0:T(8,128)S(1)}, u32[]{:S(2)}) copy-start(f32[256,3584]{1,0:T(8,128)S(1)} %get-tuple-element.11.merged_ref) | copy-start | bytes 11010052
  9.3 1.2 %collective-permute-start = (f32[16,256]{1,0:T(8,128)S(1)}, f32[16,256]{1,0:T(8,128)S(1)}, u32[]{:S(2)}, u32[]{:S(2)}) collective-permute-start(f32[16,256]{1,0:T(8,128)S(1)} %dynamic-slice_bitcast_fusion), channel_id=1, source_target_pairs={{0,1},{1,0},{2,3},{3,2},{4,5},{5,4},{6,7},{7,6},{8,9},{9,8},{10,11... | collective-permute-start | bytes 49160 | tf_op jit(solution)/shard_map/ppermute | solution.py:164
  42.9 1.3 %collective-permute-start.1 = (f32[16,256]{1,0:T(8,128)S(1)}, f32[16,256]{1,0:T(8,128)S(1)}, u32[]{:S(2)}, u32[]{:S(2)}) collective-permute-start(f32[16,256]{1,0:T(8,128)S(1)} %reduce_sum.28), channel_id=1, source_target_pairs={{0,1},{1,0},{2,3},{3,2},{4,5},{5,4},{6,7},{7,6},{8,9},{9,8},{10,11... | collective-permute-start | bytes 49160 | tf_op jit(solution)/shard_map/ppermute | solution.py:164
  50.3 2.0 %copy-start.1 = (f32[256,3584]{1,0:T(8,128)S(1)}, f32[256,3584]{1,0:T(8,128)}, u32[]{:S(2)}) copy-start(f32[256,3584]{1,0:T(8,128)} %copy-done) | copy-start | bytes 11010052
  53.7 9.0 %collective-permute-start.2 = (f32[8,3584]{1,0:T(8,128)S(1)}, f32[8,3584]{1,0:T(8,128)S(1)}, u32[]{:S(2)}, u32[]{:S(2)}) collective-permute-start(f32[8,3584]{1,0:T(8,128)S(1)} %get-tuple-element.13), channel_id=1, source_target_pairs={{0,64},{64,128},{128,192},{192,0},{1,65},{65,129},{129,193},{193,1... | collective-permute-start | bytes 344072 | tf_op jit(solution)/shard_map/ppermute | solution.py:164
  53.8 8.9 %collective-permute-start.3 = (f32[8,3584]{1,0:T(8,128)S(1)}, f32[8,3584]{1,0:T(8,128)S(1)}, u32[]{:S(2)}, u32[]{:S(2)}) collective-permute-start(f32[8,3584]{1,0:T(8,128)S(1)} %get-tuple-element.14), channel_id=1, source_target_pairs={{0,128},{64,192},{128,0},{192,64},{1,129},{65,193},{129,1},{193,65... | collective-permute-start | bytes 344072 | tf_op jit(solution)/shard_map/ppermute | solution.py:164
  56.1 7.2 %collective-permute-start.4 = (f32[8,3584]{1,0:T(8,128)S(1)}, f32[8,3584]{1,0:T(8,128)S(1)}, u32[]{:S(2)}, u32[]{:S(2)}) collective-permute-start(f32[8,3584]{1,0:T(8,128)S(1)} %get-tuple-element.15), channel_id=1, source_target_pairs={{0,192},{64,0},{128,64},{192,128},{1,193},{65,1},{129,65},{193,129... | collective-permute-start | bytes 344072 | tf_op jit(solution)/shard_map/ppermute | solution.py:164
  86.2 6.0 %collective-permute-start.7 = (f32[8,3584]{1,0:T(8,128)S(1)}, f32[8,3584]{1,0:T(8,128)S(1)}, u32[]{:S(2)}, u32[]{:S(2)}) collective-permute-start(f32[8,3584]{1,0:T(8,128)S(1)} %bitcast.33), channel_id=1, source_target_pairs={{0,192},{64,0},{128,64},{192,128},{1,193},{65,1},{129,65},{193,129... | collective-permute-start | bytes 344072 | tf_op jit(solution)/shard_map/ppermute | solution.py:164
  88.6 6.4 %collective-permute-start.6 = (f32[8,3584]{1,0:T(8,128)S(1)}, f32[8,3584]{1,0:T(8,128)S(1)}, u32[]{:S(2)}, u32[]{:S(2)}) collective-permute-start(f32[8,3584]{1,0:T(8,128)S(1)} %bitcast.34), channel_id=1, source_target_pairs={{0,128},{64,192},{128,0},{192,64},{1,129},{65,193},{129,1},{193,65... | collective-permute-start | bytes 344072 | tf_op jit(solution)/shard_map/ppermute | solution.py:164
  88.6 7.2 %collective-permute-start.5 = (f32[8,3584]{1,0:T(8,128)S(1)}, f32[8,3584]{1,0:T(8,128)S(1)}, u32[]{:S(2)}, u32[]{:S(2)}) collective-permute-start(f32[8,3584]{1,0:T(8,128)S(1)} %bitcast.35), channel_id=1, source_target_pairs={{0,64},{64,128},{128,192},{192,0},{1,65},{65,129},{129,193},{193,1... | collective-permute-start | bytes 344072 | tf_op jit(solution)/shard_map/ppermute | solution.py:164
  95.9 2.0 %copy-start.2 = (f32[256,3584]{1,0:T(8,128)S(1)}, f32[256,3584]{1,0:T(8,128)}, u32[]{:S(2)}) copy-start(f32[256,3584]{1,0:T(8,128)} %copy-done) | copy-start | bytes 11010052

commit v2 on v0

v2 whole, which is shorter than its diff:
```python
import functools

import jax
import jax.numpy as jnp
from jax import lax
from jax.experimental import pallas as pl
from jax.experimental.pallas import tpu as pltpu
from jax.sharding import Mesh
from jax.sharding import PartitionSpec as P
F32 = jnp.float32
BF16 = jnp.bfloat16
MiB = 1024 * 1024

def halves(value):
    high = value.astype(BF16)
    return high, (value - high.astype(F32)).astype(BF16)

def dot(a, b, ca, cb):
    return lax.dot_general(a, b, (((ca,), (cb,)), ((), ())), preferred_element_type=F32)

def spans(cuts):
    start = 0
    for size in cuts:
        yield pl.ds(start, size)
        start += size

def project_kernel(cuts, inner, core, gradient, feedback, basis, merged, mine, other, p_buf, g_buf, f_buf, b_buf, g_sem, f_sem, b_sem):
    rank = basis.shape[0]
    fetch_basis = pltpu.make_async_copy(basis, b_buf, b_sem)
    fetch_basis.start()
    fetch = []
    for i, part in enumerate(spans(cuts)):
        pair = (pltpu.make_async_copy(feedback.at[part], f_buf.at[part], f_sem.at[i]),
                pltpu.make_async_copy(gradient.at[part], g_buf.at[part], g_sem.at[i]))
        for c in pair: c.start()
        fetch.append(pair)
    fetch_basis.wait()
    w_high, w_low = halves(b_buf[...])
    stack = jnp.concatenate([w_high, w_low], axis=0)
    terms = []
    cols = merged.shape[1]
    for i, part in enumerate(spans(cuts)):
        for c in fetch[i]: c.wait()
        total = None
        for k in range(0, cols, inner):
            span = pl.ds(k, inner)
            value = g_buf[part, span].astype(F32) + f_buf[part, span]
            merged[part, span] = value
            high, low = halves(value)
            both = dot(high, stack[:, k : k + inner], 1, 1)
            term = both[:, :rank] + both[:, rank:] + dot(low, w_high[:, k : k + inner], 1, 1)
            total = term if total is None else total + term
        terms.append(total)
    p_buf[...] = jnp.concatenate(terms, axis=0).T
    half = rank // 2
    mine[...] = p_buf[pl.ds(pl.multiple_of(core[0] * half, 8), half)]
    other[...] = p_buf[pl.ds(pl.multiple_of((1 - core[0]) * half, 8), half)]

def project(core, gradient, feedback, basis, cuts, inner=512, limit=24):
    rows, cols = feedback.shape
    rank = basis.shape[0]
    hbm = [pltpu.with_memory_space_constraint(x, pltpu.HBM) for x in (gradient, feedback, basis)]
    count = len(cuts)
    return pl.pallas_call(
        functools.partial(project_kernel, cuts, inner),
        in_specs=[pl.BlockSpec(memory_space=pltpu.SMEM)] + [pl.BlockSpec(memory_space=pltpu.HBM)] * 3,
        out_specs=[pl.BlockSpec(memory_space=pltpu.VMEM)] * 3,
        out_shape=[pltpu.VMEM((rows, cols), F32)] + [pltpu.VMEM((rank // 2, rows), F32)] * 2,
        scratch_shapes=[
            pltpu.VMEM((rank, rows), F32),
            pltpu.VMEM((rows, cols), BF16), pltpu.VMEM((rows, cols), F32), pltpu.VMEM((rank, cols), F32),
            pltpu.SemaphoreType.DMA((count,)), pltpu.SemaphoreType.DMA((count,)), pltpu.SemaphoreType.DMA],
        compiler_params=pltpu.CompilerParams(vmem_limit_bytes=limit * MiB),
        name="project",
    )(core, *hbm)

def factor_kernel(chunk, place, projected, merged, *outs):
    rank, count = projected.shape[0], len(outs)
    depth = rank // count
    rows = [projected[pl.ds(pl.multiple_of(lax.rem(place[0] + k, count) * depth, 8), depth)] for k in range(count)]
    p_high, p_low = halves(jnp.concatenate(rows, axis=0))
    stack = jnp.concatenate([p_high, p_low], axis=0)
    for i in range(merged.shape[1] // chunk):
        part = pl.ds(i * chunk, chunk)
        high, low = halves(merged[:, part])
        both = dot(stack, high, 1, 0)
        term = both[:rank] + both[rank:] + dot(p_high, low, 1, 0)
        for k, out in enumerate(outs):
            if len(out.shape) == 3:
                out[:, 0, part] = term[k * depth : (k + 1) * depth]
            else:
                out[:, part] = term[k * depth : (k + 1) * depth]

def partial_factor(place, projected, merged, shapes, chunk=896, limit=16):
    merged = pltpu.with_memory_space_constraint(merged, pltpu.VMEM)
    return pl.pallas_call(
        functools.partial(factor_kernel, chunk),
        in_specs=[pl.BlockSpec(memory_space=pltpu.SMEM)] + [pl.BlockSpec(memory_space=pltpu.VMEM)] * 2,
        out_specs=[pl.BlockSpec(memory_space=pltpu.VMEM)] * len(shapes),
        out_shape=[jax.ShapeDtypeStruct(shape, F32) for shape in shapes],
        compiler_params=pltpu.CompilerParams(vmem_limit_bytes=limit * MiB),
        name="partial_factor",
    )(place, projected, merged)

def rebuild_kernel(scale, cuts, place, basis, merged, *refs):
    *factors, approx, updated, a_buf, u_buf, a_sem, u_sem = refs
    count = len(factors)
    depth = basis.shape[0] // count
    rows = [basis[pl.ds(pl.multiple_of(lax.rem(place[0] + count - k, count) * depth, 8), depth)] for k in range(count)]
    b_high, b_low = halves(jnp.concatenate(rows, axis=0))
    left = jnp.concatenate([b_high, b_high, b_low], axis=0).T
    f_high, f_low = halves(jnp.concatenate([f[...] for f in factors], axis=0))
    right = jnp.concatenate([f_high, f_low, f_high], axis=0)
    copies = []
    for i, part in enumerate(spans(cuts)):
        value = dot(left[part.start : part.start + part.size], right, 1, 0)
        a_buf[part] = value.astype(BF16)
        u_buf[part] = merged[part] - value * scale
        for c in (pltpu.make_async_copy(u_buf.at[part], updated.at[part], u_sem.at[i]),
                  pltpu.make_async_copy(a_buf.at[part], approx.at[part], a_sem.at[i])):
            c.start()
            copies.append(c)
    for c in copies: c.wait()

def rebuild(place, basis, merged, factors, replicas, cuts, limit=24):
    rows, cols = merged.shape
    count = len(cuts)
    merged = pltpu.with_memory_space_constraint(merged, pltpu.VMEM)
    return pl.pallas_call(
        functools.partial(rebuild_kernel, 1.0 / replicas, cuts),
        in_specs=[pl.BlockSpec(memory_space=pltpu.SMEM)] + [pl.BlockSpec(memory_space=pltpu.VMEM)] * (2 + len(factors)),
        out_specs=[pl.BlockSpec(memory_space=pltpu.HBM)] * 2,
        out_shape=[pltpu.HBM((rows, cols), BF16), pltpu.HBM((rows, cols), F32)],
        scratch_shapes=[pltpu.VMEM((rows, cols), BF16), pltpu.VMEM((rows, cols), F32),
                        pltpu.SemaphoreType.DMA((count,)), pltpu.SemaphoreType.DMA((count,))],
        compiler_params=pltpu.CompilerParams(vmem_limit_bytes=limit * MiB),
        name="rebuild",
    )(place, basis, merged, *factors)

def solve_kernel(projected_ref, out_ref):
    p = projected_ref[...]
    rank = p.shape[0]
    exact = functools.partial(lax.dot_general, precision=lax.Precision.HIGHEST, preferred_element_type=F32)
    gram = exact(p, p, (((1,), (1,)), ((), ())))
    eye = (lax.broadcasted_iota(jnp.int32, (rank, rank), 0) == lax.broadcasted_iota(jnp.int32, (rank, rank), 1)).astype(F32)
    state = jnp.concatenate([gram, eye], axis=1)
    row_id = lax.broadcasted_iota(jnp.int32, (rank, 1), 0)
    inverse_pivots = jnp.zeros((rank, 1), F32)
    for k in range(rank):
        row = state[k : k + 1, :]
        inverse = 1.0 / state[k : k + 1, k : k + 1]
        inverse_pivots = jnp.where(row_id == k, inverse, inverse_pivots)
        if k + 1 < rank:
            multiplier = jnp.where(row_id > k, state[:, k : k + 1] * inverse, 0.0)
            state = state - multiplier * row
    unit = state[:, rank:]
    basis = exact(unit, p, (((1,), (0,)), ((), ()))) * inverse_pivots
    out_ref[...] = exact(unit, basis, (((0,), (0,)), ((), ())))

def solve(projected):
    return pl.pallas_call(
        solve_kernel,
        out_shape=jax.ShapeDtypeStruct(projected.shape, F32),
        compiler_params=pltpu.CompilerParams(vmem_limit_bytes=4 * MiB),
        name="solve",
    )(projected)


def rotate(x, axis, size, step):
    return lax.ppermute(x, axis, [(i, (i + step) % size) for i in range(size)])


def spread(x, axes, size):
    return lax.all_to_all(jnp.broadcast_to(x[None], (size,) + x.shape), axes, 0, 0)


def added(stacked):
    return functools.reduce(jnp.add, [stacked[i] for i in range(stacked.shape[0])])


def sum_over(x, axes, size):
    return added(spread(x, axes, size))


def sum_around(x, axis, size):
    arrived = [rotate(x, axis, size, k) for k in range(1, size)]
    return functools.reduce(jnp.add, arrived, x)


def sum_everywhere(mine, other, sizes):
    mine = mine + rotate(other, "core", 2, 1)
    mine = sum_over(mine, "z", sizes["z"])
    mine = sum_over(mine, ("y", "x"), sizes["y"] * sizes["x"])
    return jnp.concatenate([mine, rotate(mine, "core", 2, 1)])


def sum_factor(pieces, sizes):
    y, z = sizes["y"], sizes["z"]
    depth, cols = pieces[0].shape
    arrived = [rotate(pieces[k], "y", y, k) for k in range(1, y)]
    mine = functools.reduce(jnp.add, arrived, pieces[0])
    arrived = lax.all_to_all(mine.reshape(z, depth // z, cols), "z", 0, 0)
    whole = spread(added(arrived), "z", z).reshape(depth, cols)
    return [whole] + [rotate(whole, "y", y, k) for k in range(1, y)]


def shapes_of(rank, cols, sizes):
    return [(rank // sizes["y"], cols)] * sizes["y"]


def local(sizes, gradient, feedback, warm_basis):
    replicas = sizes["y"] * sizes["z"]
    rank, cols = warm_basis.shape
    core = lax.axis_index("core").reshape(1)
    place = lax.axis_index("y").reshape(1)
    core, place = lax.optimization_barrier((core, place))
    merged, mine, other = project(core, gradient[0], feedback[0], warm_basis, (128, 128))
    projected = sum_everywhere(mine, other, sizes)
    pieces = partial_factor(place, projected, merged, shapes_of(rank, cols, sizes))
    basis = solve(projected)
    factors = sum_factor(pieces, sizes)
    approx, updated = rebuild(place, basis, merged, factors, replicas, (64, 64, 64, 64))
    return (approx, updated[None])


def solution(mesh):
    sizes = {"y": 4, "z": 8, "x": 4, "core": 2}
    inner = Mesh(mesh.devices.reshape(tuple(sizes.values())), tuple(sizes))
    dp, mp = ("y", "z"), ("x", "core")
    return jax.shard_map(
        functools.partial(local, sizes),
        mesh=inner,
        in_specs=(P(dp, None, mp), P(dp, None, mp), P(None, mp)),
        out_specs=(P(None, mp), P(dp, None, mp)),
        check_vma=False,
    )
```

time: 264 us -> 85.1 us (0.32)
  waiting for transfers between devices: 144 us -> 11.3 us
  blocking collectives: 78.9 us -> 54.8 us
  matrix products: 18.2 us -> 0 us
  between operations: 14.1 us -> 0.73 us
  Pallas kernels: 0 us -> 10.5 us
  starting transfers between devices: 0.04 us -> 7.11 us
  other arithmetic: 6.69 us -> 0.14 us
    psum x1 -> x0, waiting for transfers between devices: 144 us -> none  [local(): lax.psum(jnp.dot(ortho_basis, merged, precision=lax.Precision.HIGHEST), '...]
    psum x1 -> x0, blocking collectives: 78.9 us -> none  [local(): summed = lax.psum(partial_value, ('dp', 'mp'))]
    all_to_all x0 -> x4, blocking collectives: none -> 54.8 us  [the longest x3 43.5 us: spread(): lax.all_to_all(jnp.broadcast_to(x[None], (size,) + x.shape), axes, 0, 0)]
    dot_general x4 -> x0, matrix products: 18 us -> none  [the longest x1 6.8 us: rebuild(): lax.dot_general(ortho_basis, factor, (((0,), (0,)), ((), ())), precision=...]
    ppermute x0 -> x8, waiting for transfers between devices: none -> 11.3 us  [rotate(): return lax.ppermute(x, axis, [(i, (i + step) % size) for i in range(size)])]
    pallas_call x0 -> x4, Pallas kernels: none -> 10.5 us  [the longest x1 3.58 us: project(): pl.pallas_call(functools.partial(project_kernel, cuts, inner), in_specs=[...]
    ppermute x0 -> x8, starting transfers between devices: none -> 7.11 us  [rotate(): return lax.ppermute(x, axis, [(i, (i + step) % size) for i in range(size)])]
    another operation x5 -> x0, other arithmetic: 6.68 us -> none  [the longest x3 3.6 us: local(): factor_low = jnp.linalg.cholesky(gram_sum)]
  transfers between devices with their start and end apart: 1 -> 8, of which waited for: 1 -> 6; matrix products, arithmetic and copies ran while one was open for 0% -> 0% of each run, Pallas kernels for 0% -> 4%
where the time goes in v2:
time: 85.1 us; the launch traced here: 84.8 us
  blocking collectives  54.8 us (64%)
  waiting for transfers between devices  11.3 us (13%)
  Pallas kernels  10.5 us (12%)
  starting transfers between devices  7.11 us (8%)
    all_to_all x3, blocking collectives, spread(): lax.all_to_all(jnp.broadcast_to(x[None], (size,) + x.shape), axes, 0, 0)  43.5 us
    ppermute x8, waiting for transfers between devices, rotate(): return lax.ppermute(x, axis, [(i, (i + step) % size) for i in range(size)])  11.3 us
    all_to_all x1, blocking collectives, sum_factor(): arrived = lax.all_to_all(mine.reshape(z, depth // z, cols), 'z', 0, 0)  11.3 us
    ppermute x8, starting transfers between devices, rotate(): return lax.ppermute(x, axis, [(i, (i + step) % size) for i in range(size)])  7.11 us
    pallas_call x1, Pallas kernels, project(): pl.pallas_call(functools.partial(project_kernel, cuts, inner), in_specs=[...  3.58 us
    pallas_call x1, Pallas kernels, solve(): pl.pallas_call(solve_kernel, out_shape=jax.ShapeDtypeStruct(projected.sha...  3.33 us
    pallas_call x1, Pallas kernels, rebuild(): pl.pallas_call(functools.partial(rebuild_kernel, 1.0 / replicas, cuts), i...  2.84 us
  transfers between devices with their start and end apart: 8, of which 6 were waited for; matrix products, arithmetic and copies ran while one was open for 0% of the time, Pallas kernels for 4%

profile of v2, /device:TPU:2, one launch (start us, length us, event | category | flops | bytes accessed | tf_op | source)
XLA Modules:
  0.0 84.8 jit_solution(604124948899687678)
XLA Ops:
  0.6 3.6 %project.1 = (f32[256,3584]{1,0:T(8,128)S(1)}, f32[16,256]{1,0:T(8,128)S(1)}, f32[16,256]{1,0:T(8,128)S(1)}) custom-call(s32[1]{0:T(128)} %bitcast.core, bf16[256,3584]{1,0:T(8,128)(2,1)} %bitcast.19, f32[256,3584]{1,0:T(8,128)} %bitcast.18, f32[32,3584]{1,0:T(8,128)} %basis.1), custom_call_target="tpu_custom_call" | custom-call | tf_op jit(solution)/shard_map/project/pallas_call | solution.py:64
  4.2 0.1 collective-permute-start
  4.3 1.2 %collective-permute-done = f32[16,256]{1,0:T(8,128)S(1)} collective-permute-done((f32[16,256]{1,0:T(8,128)S(1)}, f32[16,256]{1,0:T(8,128)S(1)}, u32[]{:S(2)}, u32[]{:S(2)}) %collective-permute-start) | collective-permute-done | bytes 16416 | tf_op jit(solution)/shard_map/ppermute | solution.py:170
  5.5 17.7 %all_to_all.20 = f32[8,16,256]{2,1,0:T(8,128)S(1)} all-to-all(f32[8,16,256]{2,1,0:T(8,128)S(1)} %broadcast_in_dim.12), channel_id=1, replica_groups=mesh['y'=4,'z'=8,'x'=4,'core'=2] {'z'}, dimensions={0} | all-to-all | bytes 262144 | tf_op jit(solution)/shard_map/all_to_all | solution.py:174
  23.2 14.6 %all_to_all.21 = f32[16,16,256]{2,1,0:T(8,128)S(1)} all-to-all(f32[16,16,256]{2,1,0:T(8,128)S(1)} %broadcast_in_dim.27), channel_id=1, replica_groups=mesh['y'=4,'z'=8,'x'=4,'core'=2] {'y','x'}, dimensions={0} | all-to-all | bytes 524288 | tf_op jit(solution)/shard_map/all_to_all | solution.py:174
  37.8 0.1 collective-permute-start.1
  37.9 1.2 %collective-permute-done.1 = f32[16,256]{1,0:T(8,128)S(1)} collective-permute-done((f32[16,256]{1,0:T(8,128)S(1)}, f32[16,256]{1,0:T(8,128)S(1)}, u32[]{:S(2)}, u32[]{:S(2)}) %collective-permute-start.1) | collective-permute-done | bytes 16416 | tf_op jit(solution)/shard_map/ppermute | solution.py:170
  39.1 0.8 partial_factor.1
  39.9 0.1 collective-permute-start.2
  40.0 2.3 %collective-permute-start.3 = (f32[8,3584]{1,0:T(8,128)S(1)}, f32[8,3584]{1,0:T(8,128)S(1)}, u32[]{:S(2)}, u32[]{:S(2)}) collective-permute-start(f32[8,3584]{1,0:T(8,128)S(1)} %get-tuple-element.20), channel_id=1, source_target_pairs={{0,128},{64,192},{128,0},{192,64},{1,129},{65,193},{129,1},{193,65... | collective-permute-start | bytes 344072 | tf_op jit(solution)/shard_map/ppermute | solution.py:170
  42.3 1.2 %collective-permute-start.4 = (f32[8,3584]{1,0:T(8,128)S(1)}, f32[8,3584]{1,0:T(8,128)S(1)}, u32[]{:S(2)}, u32[]{:S(2)}) collective-permute-start(f32[8,3584]{1,0:T(8,128)S(1)} %get-tuple-element.21), channel_id=1, source_target_pairs={{0,192},{64,0},{128,64},{192,128},{1,193},{65,1},{129,65},{193,129... | collective-permute-start | bytes 344072 | tf_op jit(solution)/shard_map/ppermute | solution.py:170
  43.5 5.4 %collective-permute-done.2 = f32[8,3584]{1,0:T(8,128)S(1)} collective-permute-done((f32[8,3584]{1,0:T(8,128)S(1)}, f32[8,3584]{1,0:T(8,128)S(1)}, u32[]{:S(2)}, u32[]{:S(2)}) %collective-permute-start.2) | collective-permute-done | bytes 114720 | tf_op jit(solution)/shard_map/ppermute | solution.py:170
  48.9 0.0 collective-permute-done.3
  48.9 0.6 collective-permute-done.4
  49.5 0.1 copy.5
  49.6 11.3 %all_to_all.22 = f32[8,1,3584]{2,1,0:T(1,128)S(1)} all-to-all(f32[8,1,3584]{2,1,0:T(1,128)S(1)} %copy.5), channel_id=1, replica_groups=mesh['y'=4,'z'=8,'x'=4,'core'=2] {'z'}, dimensions={0} | all-to-all | bytes 229376 | tf_op jit(solution)/shard_map/all_to_all | solution.py:202
  60.9 0.1 fusion.2
  61.0 0.1 broadcast_in_dim.29
  61.1 11.3 %all_to_all.23 = f32[8,1,3584]{2,1,0:T(1,128)S(1)} all-to-all(f32[8,1,3584]{2,1,0:T(1,128)S(1)} %broadcast_in_dim.29), channel_id=1, replica_groups=mesh['y'=4,'z'=8,'x'=4,'core'=2] {'z'}, dimensions={0} | all-to-all | bytes 229376 | tf_op jit(solution)/shard_map/all_to_all | solution.py:174
  72.4 2.4 %collective-permute-start.7 = (f32[8,3584]{1,0:T(8,128)S(1)}, f32[8,3584]{1,0:T(8,128)S(1)}, u32[]{:S(2)}, u32[]{:S(2)}) collective-permute-start(f32[8,3584]{1,0:T(8,128)S(1)} %bitcast.14), channel_id=1, source_target_pairs={{0,192},{64,0},{128,64},{192,128},{1,193},{65,1},{129,65},{193,129... | collective-permute-start | bytes 344072 | tf_op jit(solution)/shard_map/ppermute | solution.py:170
  74.8 0.0 collective-permute-start.6
  74.8 1.0 %collective-permute-start.5 = (f32[8,3584]{1,0:T(8,128)S(1)}, f32[8,3584]{1,0:T(8,128)S(1)}, u32[]{:S(2)}, u32[]{:S(2)}) collective-permute-start(f32[8,3584]{1,0:T(8,128)S(1)} %bitcast.16), channel_id=1, source_target_pairs={{0,64},{64,128},{128,192},{192,0},{1,65},{65,129},{129,193},{193,1... | collective-permute-start | bytes 344072 | tf_op jit(solution)/shard_map/ppermute | solution.py:170
  75.7 3.3 %solve.1.basis = f32[32,256]{1,0:T(8,128)S(1)} custom-call(f32[32,256]{1,0:T(8,128)S(1)} %pad_maximum_fusion.projected_ref.projected), custom_call_target="tpu_custom_call" | custom-call | tf_op jit(solution)/shard_map/solve/pallas_call | solution.py:161
  79.1 0.0 collective-permute-done.7.refs_3_
  79.1 2.1 %collective-permute-done.6.refs_2_ = f32[8,3584]{1,0:T(8,128)S(1)} collective-permute-done((f32[8,3584]{1,0:T(8,128)S(1)}, f32[8,3584]{1,0:T(8,128)S(1)}, u32[]{:S(2)}, u32[]{:S(2)}) %collective-permute-start.6) | collective-permute-done | bytes 114720 | tf_op jit(solution)/shard_map/ppermute | solution.py:170
  81.2 0.8 collective-permute-done.5.refs_1_
  82.0 2.8 %rebuild.1 = (bf16[256,3584]{1,0:T(8,128)(2,1)}, f32[256,3584]{1,0:T(8,128)}) custom-call(s32[1]{0:T(128)} %bitcast.1.place, f32[32,256]{1,0:T(8,128)S(1)} %solve.1.basis, f32[256,3584]{1,0:T(8,128)S(1)} %get-tuple-element.17.merged, f32[8,3584]{1,0:T(8,128)S(1)} %bitcast.17, f32[8,3584]{1,0:T(8,128)S(1)} %collective-permute-done.5.refs_1_, ...), custom_call_target="tpu_custom_call" | custom-call | tf_op jit(solution)/shard_map/rebuild/pallas_call | solution.py:129
  (8 shorter events, 0.1 us)
Async XLA Ops:
  4.2 1.3 %collective-permute-start = (f32[16,256]{1,0:T(8,128)S(1)}, f32[16,256]{1,0:T(8,128)S(1)}, u32[]{:S(2)}, u32[]{:S(2)}) collective-permute-start(f32[16,256]{1,0:T(8,128)S(1)} %get-tuple-element.16), channel_id=1, source_target_pairs={{0,1},{1,0},{2,3},{3,2},{4,5},{5,4},{6,7},{7,6},{8,9},{9,8},{10,11... | collective-permute-start | bytes 49160 | tf_op jit(solution)/shard_map/ppermute | solution.py:170
  37.8 1.3 %collective-permute-start.1 = (f32[16,256]{1,0:T(8,128)S(1)}, f32[16,256]{1,0:T(8,128)S(1)}, u32[]{:S(2)}, u32[]{:S(2)}) collective-permute-start(f32[16,256]{1,0:T(8,128)S(1)} %fusion), channel_id=1, source_target_pairs={{0,1},{1,0},{2,3},{3,2},{4,5},{5,4},{6,7},{7,6},{8,9},{9,8},{10,11... | collective-permute-start | bytes 49160 | tf_op jit(solution)/shard_map/ppermute | solution.py:170
  39.9 9.0 %collective-permute-start.2 = (f32[8,3584]{1,0:T(8,128)S(1)}, f32[8,3584]{1,0:T(8,128)S(1)}, u32[]{:S(2)}, u32[]{:S(2)}) collective-permute-start(f32[8,3584]{1,0:T(8,128)S(1)} %get-tuple-element.19), channel_id=1, source_target_pairs={{0,64},{64,128},{128,192},{192,0},{1,65},{65,129},{129,193},{193,1... | collective-permute-start | bytes 344072 | tf_op jit(solution)/shard_map/ppermute | solution.py:170
  40.0 8.9 %collective-permute-start.3 = (f32[8,3584]{1,0:T(8,128)S(1)}, f32[8,3584]{1,0:T(8,128)S(1)}, u32[]{:S(2)}, u32[]{:S(2)}) collective-permute-start(f32[8,3584]{1,0:T(8,128)S(1)} %get-tuple-element.20), channel_id=1, source_target_pairs={{0,128},{64,192},{128,0},{192,64},{1,129},{65,193},{129,1},{193,65... | collective-permute-start | bytes 344072 | tf_op jit(solution)/shard_map/ppermute | solution.py:170
  42.3 7.2 %collective-permute-start.4 = (f32[8,3584]{1,0:T(8,128)S(1)}, f32[8,3584]{1,0:T(8,128)S(1)}, u32[]{:S(2)}, u32[]{:S(2)}) collective-permute-start(f32[8,3584]{1,0:T(8,128)S(1)} %get-tuple-element.21), channel_id=1, source_target_pairs={{0,192},{64,0},{128,64},{192,128},{1,193},{65,1},{129,65},{193,129... | collective-permute-start | bytes 344072 | tf_op jit(solution)/shard_map/ppermute | solution.py:170
  72.4 6.7 %collective-permute-start.7 = (f32[8,3584]{1,0:T(8,128)S(1)}, f32[8,3584]{1,0:T(8,128)S(1)}, u32[]{:S(2)}, u32[]{:S(2)}) collective-permute-start(f32[8,3584]{1,0:T(8,128)S(1)} %bitcast.14), channel_id=1, source_target_pairs={{0,192},{64,0},{128,64},{192,128},{1,193},{65,1},{129,65},{193,129... | collective-permute-start | bytes 344072 | tf_op jit(solution)/shard_map/ppermute | solution.py:170
  74.8 6.4 %collective-permute-start.6 = (f32[8,3584]{1,0:T(8,128)S(1)}, f32[8,3584]{1,0:T(8,128)S(1)}, u32[]{:S(2)}, u32[]{:S(2)}) collective-permute-start(f32[8,3584]{1,0:T(8,128)S(1)} %bitcast.15), channel_id=1, source_target_pairs={{0,128},{64,192},{128,0},{192,64},{1,129},{65,193},{129,1},{193,65... | collective-permute-start | bytes 344072 | tf_op jit(solution)/shard_map/ppermute | solution.py:170
  74.8 7.2 %collective-permute-start.5 = (f32[8,3584]{1,0:T(8,128)S(1)}, f32[8,3584]{1,0:T(8,128)S(1)}, u32[]{:S(2)}, u32[]{:S(2)}) collective-permute-start(f32[8,3584]{1,0:T(8,128)S(1)} %bitcast.16), channel_id=1, source_target_pairs={{0,64},{64,128},{128,192},{192,0},{1,65},{65,129},{129,193},{193,1... | collective-permute-start | bytes 344072 | tf_op jit(solution)/shard_map/ppermute | solution.py:170

commit v3 on v2

v3 whole, which is shorter than its diff:
```python
import functools

import jax
import jax.numpy as jnp
from jax import lax
from jax.experimental import pallas as pl
from jax.experimental.pallas import tpu as pltpu
from jax.sharding import Mesh
from jax.sharding import PartitionSpec as P

F32 = jnp.float32
BF16 = jnp.bfloat16
MiB = 1024 * 1024
VMEM = pl.BlockSpec(memory_space=pltpu.VMEM)
HBM = pl.BlockSpec(memory_space=pltpu.HBM)


def halves(value):
    high = value.astype(BF16)
    return high, (value - high.astype(F32)).astype(BF16)


def dot(a, b, ca, cb):
    return lax.dot_general(a, b, (((ca,), (cb,)), ((), ())), preferred_element_type=F32)


def params(limit):
    return pltpu.CompilerParams(vmem_limit_bytes=limit * MiB)


def spans(cuts):
    start = 0
    for size in cuts:
        yield pl.ds(start, size)
        start += size


def column_block(place, k, count, width):
    return pl.ds(pl.multiple_of(lax.rem(place + k, count) * width, 128), width)


def project_kernel(cuts, inner, gradient, feedback, basis, *refs):
    merged, mine, other, p_buf, g_buf, f_buf, b_buf, g_sem, f_sem, b_sem = refs
    core = lax.axis_index("core")
    rank, cols = basis.shape
    fetch_basis = pltpu.make_async_copy(basis, b_buf, b_sem)
    fetch_basis.start()
    fetch = []
    for i, part in enumerate(spans(cuts)):
        pair = (
            pltpu.make_async_copy(feedback.at[part], f_buf.at[part], f_sem.at[i]),
            pltpu.make_async_copy(gradient.at[part], g_buf.at[part], g_sem.at[i]),
        )
        for copy in pair:
            copy.start()
        fetch.append(pair)
    fetch_basis.wait()
    w_high, w_low = halves(b_buf[...])
    stack = jnp.concatenate([w_high, w_low], axis=0)
    terms = []
    for i, part in enumerate(spans(cuts)):
        for copy in fetch[i]:
            copy.wait()
        total = None
        for at in range(0, cols, inner):
            span = pl.ds(at, inner)
            value = g_buf[part, span].astype(F32) + f_buf[part, span]
            merged[part, span] = value
            high, low = halves(value)
            both = dot(high, stack[:, at : at + inner], 1, 1)
            term = both[:, :rank] + both[:, rank:]
            term = term + dot(low, w_high[:, at : at + inner], 1, 1)
            total = term if total is None else total + term
        terms.append(total)
    p_buf[...] = jnp.concatenate(terms, axis=0).T
    half = rank // 2
    mine[...] = p_buf[pl.ds(pl.multiple_of(core * half, 8), half)]
    other[...] = p_buf[pl.ds(pl.multiple_of((1 - core) * half, 8), half)]


def project(gradient, feedback, basis, cuts=(128, 128), inner=512):
    rows, cols = feedback.shape
    rank = basis.shape[0]
    arrays = [
        pltpu.with_memory_space_constraint(x, pltpu.HBM)
        for x in (gradient, feedback, basis)
    ]
    return pl.pallas_call(
        functools.partial(project_kernel, cuts, inner),
        in_specs=[HBM] * 3,
        out_specs=[VMEM] * 3,
        out_shape=[pltpu.VMEM((rows, cols), F32)]
        + [pltpu.VMEM((rank // 2, rows), F32)] * 2,
        scratch_shapes=[
            pltpu.VMEM((rank, rows), F32),
            pltpu.VMEM((rows, cols), BF16),
            pltpu.VMEM((rows, cols), F32),
            pltpu.VMEM((rank, cols), F32),
            pltpu.SemaphoreType.DMA((len(cuts),)),
            pltpu.SemaphoreType.DMA((len(cuts),)),
            pltpu.SemaphoreType.DMA,
        ],
        compiler_params=params(20),
        name="project",
    )(*arrays)


def factor_kernel(blocks, projected, merged, out):
    rank = projected.shape[0]
    count, depth, width = out.shape
    groups = count // blocks
    p_high, p_low = halves(projected[...])
    stack = jnp.concatenate([p_high, p_low], axis=0)
    for k in range(blocks):
        high, low = halves(merged[:, k * width : (k + 1) * width])
        both = dot(stack, high, 1, 0)
        term = both[:rank] + both[rank:] + dot(p_high, low, 1, 0)
        out[k * groups : (k + 1) * groups] = term.reshape(groups, depth, width)


def partial_factor(projected, merged, blocks, shape):
    merged = pltpu.with_memory_space_constraint(merged, pltpu.VMEM)
    return pl.pallas_call(
        functools.partial(factor_kernel, blocks),
        in_specs=[VMEM] * 2,
        out_specs=VMEM,
        out_shape=jax.ShapeDtypeStruct(shape, F32),
        compiler_params=params(8),
        name="partial_factor",
    )(projected, merged)


def rebuild_kernel(scale, ahead, count, basis, merged, *refs):
    factors = refs[: len(ahead)]
    approx, updated, a_buf, u_buf, a_sem, u_sem = refs[-6:]
    rank = basis.shape[0]
    width = factors[0].shape[-1]
    place = lax.axis_index("y")
    b_high, b_low = halves(basis[...])
    left = jnp.concatenate([b_high, b_high, b_low], axis=0).T
    copies = []
    for i, (k, factor) in enumerate(zip(ahead, factors)):
        f_high, f_low = halves(factor[...].reshape(rank, width))
        value = dot(left, jnp.concatenate([f_high, f_low, f_high], axis=0), 1, 0)
        part = column_block(place, k, count, width)
        a_buf[i] = value.astype(BF16)
        u_buf[i] = merged[:, part] - value * scale
        for copy in (
            pltpu.make_async_copy(u_buf.at[i], updated.at[:, part], u_sem.at[i]),
            pltpu.make_async_copy(a_buf.at[i], approx.at[:, part], a_sem.at[i]),
        ):
            copy.start()
            copies.append(copy)
    for copy in copies:
        copy.wait()


def rebuild(basis, merged, factors, ahead, count, replicas, earlier=()):
    rows, cols = merged.shape
    width = cols // count
    merged = pltpu.with_memory_space_constraint(merged, pltpu.VMEM)
    earlier = [pltpu.with_memory_space_constraint(x, pltpu.HBM) for x in earlier]
    first = 2 + len(factors)
    return pl.pallas_call(
        functools.partial(rebuild_kernel, 1.0 / replicas, ahead, count),
        in_specs=[VMEM] * (2 + len(factors)) + [HBM] * len(earlier),
        out_specs=[HBM] * 2,
        out_shape=[pltpu.HBM((rows, cols), BF16), pltpu.HBM((rows, cols), F32)],
        input_output_aliases={first + i: i for i in range(len(earlier))},
        scratch_shapes=[
            pltpu.VMEM((len(ahead), rows, width), BF16),
            pltpu.VMEM((len(ahead), rows, width), F32),
            pltpu.SemaphoreType.DMA((len(ahead),)),
            pltpu.SemaphoreType.DMA((len(ahead),)),
        ],
        compiler_params=params(20),
        name="rebuild",
    )(basis, merged, *factors, *earlier)


def solve_kernel(projected_ref, out_ref):
    p = projected_ref[...]
    rank = p.shape[0]
    exact = functools.partial(
        lax.dot_general, precision=lax.Precision.HIGHEST, preferred_element_type=F32
    )
    gram = exact(p, p, (((1,), (1,)), ((), ())))
    eye = (
        lax.broadcasted_iota(jnp.int32, (rank, rank), 0)
        == lax.broadcasted_iota(jnp.int32, (rank, rank), 1)
    ).astype(F32)
    state = jnp.concatenate([gram, eye], axis=1)
    row_id = lax.broadcasted_iota(jnp.int32, (rank, 1), 0)
    inverse_pivots = jnp.zeros((rank, 1), F32)
    for k in range(rank):
        row = state[k : k + 1, :]
        inverse = 1.0 / state[k : k + 1, k : k + 1]
        inverse_pivots = jnp.where(row_id == k, inverse, inverse_pivots)
        if k + 1 < rank:
            multiplier = jnp.where(row_id > k, state[:, k : k + 1] * inverse, 0.0)
            state = state - multiplier * row
    unit = state[:, rank:]
    basis = exact(unit, p, (((1,), (0,)), ((), ()))) * inverse_pivots
    out_ref[...] = exact(unit, basis, (((0,), (0,)), ((), ())))


def solve(projected):
    return pl.pallas_call(
        solve_kernel,
        out_shape=jax.ShapeDtypeStruct(projected.shape, F32),
        compiler_params=params(4),
        name="solve",
    )(projected)


def rotate(x, axis, size, step):
    return lax.ppermute(x, axis, [(i, (i + step) % size) for i in range(size)])


def spread(x, axes, size):
    return lax.all_to_all(jnp.broadcast_to(x[None], (size,) + x.shape), axes, 0, 0)


def added(stacked):
    return functools.reduce(jnp.add, [stacked[i] for i in range(stacked.shape[0])])


def local(sizes, gradient, feedback, warm_basis):
    y, z, x = sizes["y"], sizes["z"], sizes["x"]
    rank, cols = warm_basis.shape
    width = cols // y
    merged, mine, other = project(gradient[0], feedback[0], warm_basis)

    mine = mine + rotate(other, "core", 2, 1)
    mine = added(spread(mine, "z", z))
    mine = added(spread(mine, ("y", "x"), y * x))
    projected = jnp.concatenate([mine, rotate(mine, "core", 2, 1)])

    factor = partial_factor(projected, merged, y, (y * z, rank // z, width))
    summed = added(lax.all_to_all(factor, ("y", "z"), 0, 0))
    whole = spread(summed, "z", z)
    arrived = [rotate(whole, "y", y, y - k) for k in range(1, y)]
    basis = solve(projected)
    build = functools.partial(rebuild, basis, merged, count=y, replicas=y * z)
    outs = build([whole], (0,))
    approx, updated = build(arrived, (1, 2, 3), earlier=outs)
    return (approx, updated[None])


def solution(mesh):
    sizes = {"y": 4, "z": 8, "x": 4, "core": 2}
    inner = Mesh(mesh.devices.reshape(tuple(sizes.values())), tuple(sizes))
    dp, mp = ("y", "z"), ("x", "core")
    return jax.shard_map(
        functools.partial(local, sizes),
        mesh=inner,
        in_specs=(P(dp, None, mp), P(dp, None, mp), P(None, mp)),
        out_specs=(P(None, mp), P(dp, None, mp)),
        check_vma=False,
    )
```

time: 85.1 us -> 83.4 us (0.980)
  blocking collectives: 54.8 us -> 64.4 us
  waiting for transfers between devices: 11.3 us -> 2.35 us
  starting transfers between devices: 7.11 us -> 4.23 us
  Pallas kernels: 10.5 us -> 11.4 us
    ppermute x8 -> x5, waiting for transfers between devices: 11.3 us -> 2.35 us  [rotate(): return lax.ppermute(x, axis, [(i, (i + step) % size) for i in range(size)])]
    all_to_all x1, blocking collectives: 11.3 us -> 19.1 us  [local(): summed = added(lax.all_to_all(factor, ('y', 'z'), 0, 0))]
    ppermute x8 -> x5, starting transfers between devices: 7.11 us -> 4.23 us  [rotate(): return lax.ppermute(x, axis, [(i, (i + step) % size) for i in range(size)])]
    all_to_all x3, blocking collectives: 43.5 us -> 45.3 us  [spread(): lax.all_to_all(jnp.broadcast_to(x[None], (size,) + x.shape), axes, 0, 0)]
    pallas_call x2 -> x3, Pallas kernels: 3.61 us -> 4.52 us  [the longest x2 3.81 us: rebuild(): pl.pallas_call(functools.partial(rebuild_kernel, 1.0 / replicas, ahead, c...]
  transfers between devices with their start and end apart: 8 -> 5, of which waited for: 6 -> 2; matrix products, arithmetic and copies ran while one was open for 0% -> 0% of each run, Pallas kernels for 4% -> 6%
where the time goes in v3:
time: 83.4 us; the launch traced here: 83.2 us
  blocking collectives  64.4 us (77%)
  Pallas kernels  11.4 us (14%)
  starting transfers between devices  4.23 us (5%)
  waiting for transfers between devices  2.35 us (3%)
    all_to_all x3, blocking collectives, spread(): lax.all_to_all(jnp.broadcast_to(x[None], (size,) + x.shape), axes, 0, 0)  45.3 us
    all_to_all x1, blocking collectives, local(): summed = added(lax.all_to_all(factor, ('y', 'z'), 0, 0))  19.1 us
    ppermute x5, starting transfers between devices, rotate(): return lax.ppermute(x, axis, [(i, (i + step) % size) for i in range(size)])  4.23 us
    pallas_call x2, Pallas kernels, rebuild(): pl.pallas_call(functools.partial(rebuild_kernel, 1.0 / replicas, ahead, c...  3.81 us
    pallas_call x1, Pallas kernels, project(): pl.pallas_call(functools.partial(project_kernel, cuts, inner), in_specs=[...  3.5 us
    pallas_call x1, Pallas kernels, solve(): pl.pallas_call(solve_kernel, out_shape=jax.ShapeDtypeStruct(projected.sha...  3.33 us
    ppermute x5, waiting for transfers between devices, rotate(): return lax.ppermute(x, axis, [(i, (i + step) % size) for i in range(size)])  2.35 us
  transfers between devices with their start and end apart: 5, of which 2 were waited for; matrix products, arithmetic and copies ran while one was open for 0% of the time, Pallas kernels for 6%

profile of v3, /device:TPU:2, one launch (start us, length us, event | category | flops | bytes accessed | tf_op | source)
XLA Modules:
  0.0 83.2 jit_solution(9648187067809586132)
XLA Ops:
  0.6 3.5 %project.1 = (f32[256,3584]{1,0:T(8,128)S(1)}, f32[16,256]{1,0:T(8,128)S(1)}, f32[16,256]{1,0:T(8,128)S(1)}) custom-call(bf16[256,3584]{1,0:T(8,128)(2,1)} %bitcast.11, f32[256,3584]{1,0:T(8,128)} %bitcast.10, f32[32,3584]{1,0:T(8,128)} %basis.1), custom_call_target="tpu_custom_call" | custom-call | tf_op jit(solution)/shard_map/project/pallas_call | solution.py:88
  4.1 0.1 collective-permute-start
  4.2 1.2 %collective-permute-done = f32[16,256]{1,0:T(8,128)S(1)} collective-permute-done((f32[16,256]{1,0:T(8,128)S(1)}, f32[16,256]{1,0:T(8,128)S(1)}, u32[]{:S(2)}, u32[]{:S(2)}) %collective-permute-start) | collective-permute-done | bytes 16416 | tf_op jit(solution)/shard_map/ppermute | solution.py:217
  5.4 17.7 %all_to_all.20 = f32[8,16,256]{2,1,0:T(8,128)S(1)} all-to-all(f32[8,16,256]{2,1,0:T(8,128)S(1)} %broadcast_in_dim.12), channel_id=1, replica_groups=mesh['y'=4,'z'=8,'x'=4,'core'=2] {'z'}, dimensions={0} | all-to-all | bytes 262144 | tf_op jit(solution)/shard_map/all_to_all | solution.py:221
  23.1 14.6 %all_to_all.21 = f32[16,16,256]{2,1,0:T(8,128)S(1)} all-to-all(f32[16,16,256]{2,1,0:T(8,128)S(1)} %broadcast_in_dim.27), channel_id=1, replica_groups=mesh['y'=4,'z'=8,'x'=4,'core'=2] {'y','x'}, dimensions={0} | all-to-all | bytes 524288 | tf_op jit(solution)/shard_map/all_to_all | solution.py:221
  37.8 0.1 collective-permute-start.1
  37.9 1.2 %collective-permute-done.1 = f32[16,256]{1,0:T(8,128)S(1)} collective-permute-done((f32[16,256]{1,0:T(8,128)S(1)}, f32[16,256]{1,0:T(8,128)S(1)}, u32[]{:S(2)}, u32[]{:S(2)}) %collective-permute-start.1) | collective-permute-done | bytes 16416 | tf_op jit(solution)/shard_map/ppermute | solution.py:217
  39.0 0.7 partial_factor.1
  39.7 19.1 %all_to_all.22 = f32[32,4,896]{2,1,0:T(4,128)S(1)} all-to-all(f32[32,4,896]{2,1,0:T(4,128)S(1)} %partial_factor.1), channel_id=1, replica_groups=mesh['y'=4,'z'=8,'x'=4,'core'=2] {'y','z'}, dimensions={0} | all-to-all | bytes 917504 | tf_op jit(solution)/shard_map/all_to_all | solution.py:240
  58.8 0.1 fusion.2
  58.9 13.1 %all_to_all.23.refs_0_ = f32[8,4,896]{2,1,0:T(4,128)S(1)} all-to-all(f32[8,4,896]{2,1,0:T(4,128)S(1)} %broadcast_in_dim.29), channel_id=1, replica_groups=mesh['y'=4,'z'=8,'x'=4,'core'=2] {'z'}, dimensions={0} | all-to-all | bytes 229376 | tf_op jit(solution)/shard_map/all_to_all | solution.py:221
  72.0 0.6 collective-permute-start.4
  72.6 2.0 %collective-permute-start.3 = (f32[8,4,896]{2,1,0:T(4,128)S(1)}, f32[8,4,896]{2,1,0:T(4,128)S(1)}, u32[]{:S(2)}, u32[]{:S(2)}) collective-permute-start(f32[8,4,896]{2,1,0:T(4,128)S(1)} %all_to_all.23.refs_0_), channel_id=1, source_target_pairs={{0,128},{64,192},{128,0},{192,64},{1,129},{65,193},{129,1},{193,65... | collective-permute-start | bytes 344072 | tf_op jit(solution)/shard_map/ppermute | solution.py:217
  74.5 1.5 %collective-permute-start.2 = (f32[8,4,896]{2,1,0:T(4,128)S(1)}, f32[8,4,896]{2,1,0:T(4,128)S(1)}, u32[]{:S(2)}, u32[]{:S(2)}) collective-permute-start(f32[8,4,896]{2,1,0:T(4,128)S(1)} %all_to_all.23.refs_0_), channel_id=1, source_target_pairs={{0,192},{64,0},{128,64},{192,128},{1,193},{65,1},{129,65},{193,129... | collective-permute-start | bytes 344072 | tf_op jit(solution)/shard_map/ppermute | solution.py:217
  76.0 3.3 %solve.1.basis = f32[32,256]{1,0:T(8,128)S(1)} custom-call(f32[32,256]{1,0:T(8,128)S(1)} %pad_maximum_fusion.projected_ref.projected), custom_call_target="tpu_custom_call" | custom-call | tf_op jit(solution)/shard_map/solve/pallas_call | solution.py:208
  79.3 1.4 %rebuild.2 = (bf16[256,3584]{1,0:T(8,128)(2,1)}, f32[256,3584]{1,0:T(8,128)}) custom-call(f32[32,256]{1,0:T(8,128)S(1)} %solve.1.basis, f32[256,3584]{1,0:T(8,128)S(1)} %get-tuple-element.11.merged, f32[8,4,896]{2,1,0:T(4,128)S(1)} %all_to_all.23.refs_0_), custom_call_target="tpu_custom_call" | custom-call | tf_op jit(solution)/shard_map/rebuild/pallas_call | solution.py:164
  80.8 0.0 collective-permute-done.4.refs_2_
  80.8 0.0 collective-permute-done.3.refs_1_
  80.8 0.0 collective-permute-done.2.refs_0_
  80.8 2.4 %rebuild.3 = (bf16[256,3584]{1,0:T(8,128)(2,1)}, f32[256,3584]{1,0:T(8,128)}) custom-call(f32[32,256]{1,0:T(8,128)S(1)} %solve.1.basis, f32[256,3584]{1,0:T(8,128)S(1)} %get-tuple-element.11.merged, f32[8,4,896]{2,1,0:T(4,128)S(1)} %collective-permute-done.2.refs_0_, ...), custom_call_target="tpu_custom_call", output_to_operand_aliasing={{0}: (5, {}), {1}: (6, {})} | custom-call | tf_op jit(solution)/shard_map/rebuild/pallas_call | solution.py:164
  (7 shorter events, 0.1 us)
Async XLA Ops:
  4.1 1.3 %collective-permute-start = (f32[16,256]{1,0:T(8,128)S(1)}, f32[16,256]{1,0:T(8,128)S(1)}, u32[]{:S(2)}, u32[]{:S(2)}) collective-permute-start(f32[16,256]{1,0:T(8,128)S(1)} %get-tuple-element.10), channel_id=1, source_target_pairs={{0,1},{1,0},{2,3},{3,2},{4,5},{5,4},{6,7},{7,6},{8,9},{9,8},{10,11... | collective-permute-start | bytes 49160 | tf_op jit(solution)/shard_map/ppermute | solution.py:217
  37.8 1.3 %collective-permute-start.1 = (f32[16,256]{1,0:T(8,128)S(1)}, f32[16,256]{1,0:T(8,128)S(1)}, u32[]{:S(2)}, u32[]{:S(2)}) collective-permute-start(f32[16,256]{1,0:T(8,128)S(1)} %fusion), channel_id=1, source_target_pairs={{0,1},{1,0},{2,3},{3,2},{4,5},{5,4},{6,7},{7,6},{8,9},{9,8},{10,11... | collective-permute-start | bytes 49160 | tf_op jit(solution)/shard_map/ppermute | solution.py:217
  72.0 8.8 %collective-permute-start.4 = (f32[8,4,896]{2,1,0:T(4,128)S(1)}, f32[8,4,896]{2,1,0:T(4,128)S(1)}, u32[]{:S(2)}, u32[]{:S(2)}) collective-permute-start(f32[8,4,896]{2,1,0:T(4,128)S(1)} %all_to_all.23.refs_0_), channel_id=1, source_target_pairs={{0,64},{64,128},{128,192},{192,0},{1,65},{65,129},{129,193},{193,1... | collective-permute-start | bytes 344072 | tf_op jit(solution)/shard_map/ppermute | solution.py:217
  72.6 8.2 %collective-permute-start.3 = (f32[8,4,896]{2,1,0:T(4,128)S(1)}, f32[8,4,896]{2,1,0:T(4,128)S(1)}, u32[]{:S(2)}, u32[]{:S(2)}) collective-permute-start(f32[8,4,896]{2,1,0:T(4,128)S(1)} %all_to_all.23.refs_0_), channel_id=1, source_target_pairs={{0,128},{64,192},{128,0},{192,64},{1,129},{65,193},{129,1},{193,65... | collective-permute-start | bytes 344072 | tf_op jit(solution)/shard_map/ppermute | solution.py:217
  74.5 6.3 %collective-permute-start.2 = (f32[8,4,896]{2,1,0:T(4,128)S(1)}, f32[8,4,896]{2,1,0:T(4,128)S(1)}, u32[]{:S(2)}, u32[]{:S(2)}) collective-permute-start(f32[8,4,896]{2,1,0:T(4,128)S(1)} %all_to_all.23.refs_0_), channel_id=1, source_target_pairs={{0,192},{64,0},{128,64},{192,128},{1,193},{65,1},{129,65},{193,129... | collective-permute-start | bytes 344072 | tf_op jit(solution)/shard_map/ppermute | solution.py:217

commit v4 on v3

--- a/solution.py
+++ b/solution.py
@@ -35,8 +35,8 @@
         start += size
 
 
-def column_block(place, k, count, width):
-    return pl.ds(pl.multiple_of(lax.rem(place + k, count) * width, 128), width)
+def column_block(index, width):
+    return pl.ds(pl.multiple_of(index * width, 128), width)
 
 
 def project_kernel(cuts, inner, gradient, feedback, basis, *refs):
@@ -130,19 +130,20 @@
     )(projected, merged)
 
 
-def rebuild_kernel(scale, ahead, count, basis, merged, *refs):
-    factors = refs[: len(ahead)]
+def rebuild_kernel(scale, across, count, basis, merged, factor, *refs):
     approx, updated, a_buf, u_buf, a_sem, u_sem = refs[-6:]
-    rank = basis.shape[0]
-    width = factors[0].shape[-1]
-    place = lax.axis_index("y")
-    b_high, b_low = halves(basis[...])
-    left = jnp.concatenate([b_high, b_high, b_low], axis=0).T
+    rank = basis.shape[1] // 3
+    groups, _, width = factor.shape
+    groups //= count
+    place = lax.axis_index("yh")
+    place = 1 - place if across else place
+    left = basis[...]
     copies = []
-    for i, (k, factor) in enumerate(zip(ahead, factors)):
-        f_high, f_low = halves(factor[...].reshape(rank, width))
+    for i in range(count):
+        f = factor[i * groups : (i + 1) * groups].reshape(rank, width)
+        f_high, f_low = halves(f)
         value = dot(left, jnp.concatenate([f_high, f_low, f_high], axis=0), 1, 0)
-        part = column_block(place, k, count, width)
+        part = column_block(2 * place + i, width)
         a_buf[i] = value.astype(BF16)
         u_buf[i] = merged[:, part] - value * scale
         for copy in (
@@ -155,30 +156,30 @@
         copy.wait()
 
 
-def rebuild(basis, merged, factors, ahead, count, replicas, earlier=()):
+def rebuild(basis, merged, factor, across, replicas, earlier=()):
     rows, cols = merged.shape
-    width = cols // count
+    width = factor.shape[2]
+    count = cols // width // 2
     merged = pltpu.with_memory_space_constraint(merged, pltpu.VMEM)
     earlier = [pltpu.with_memory_space_constraint(x, pltpu.HBM) for x in earlier]
-    first = 2 + len(factors)
-    return pl.pallas_call(
-        functools.partial(rebuild_kernel, 1.0 / replicas, ahead, count),
-        in_specs=[VMEM] * (2 + len(factors)) + [HBM] * len(earlier),
+    return pl.pallas_call(
+        functools.partial(rebuild_kernel, 1.0 / replicas, across, count),
+        in_specs=[VMEM] * 3 + [HBM] * len(earlier),
         out_specs=[HBM] * 2,
         out_shape=[pltpu.HBM((rows, cols), BF16), pltpu.HBM((rows, cols), F32)],
-        input_output_aliases={first + i: i for i in range(len(earlier))},
+        input_output_aliases={3 + i: i for i in range(len(earlier))},
         scratch_shapes=[
-            pltpu.VMEM((len(ahead), rows, width), BF16),
-            pltpu.VMEM((len(ahead), rows, width), F32),
-            pltpu.SemaphoreType.DMA((len(ahead),)),
-            pltpu.SemaphoreType.DMA((len(ahead),)),
+            pltpu.VMEM((count, rows, width), BF16),
+            pltpu.VMEM((count, rows, width), F32),
+            pltpu.SemaphoreType.DMA((count,)),
+            pltpu.SemaphoreType.DMA((count,)),
         ],
         compiler_params=params(20),
         name="rebuild",
-    )(basis, merged, *factors, *earlier)
-
-
-def solve_kernel(projected_ref, out_ref):
+    )(basis, merged, factor, *earlier)
+
+
+def solve_kernel(w, projected_ref, out_ref):
     p = projected_ref[...]
     rank = p.shape[0]
     exact = functools.partial(
@@ -191,23 +192,40 @@
     ).astype(F32)
     state = jnp.concatenate([gram, eye], axis=1)
     row_id = lax.broadcasted_iota(jnp.int32, (rank, 1), 0)
-    inverse_pivots = jnp.zeros((rank, 1), F32)
-    for k in range(rank):
-        row = state[k : k + 1, :]
-        inverse = 1.0 / state[k : k + 1, k : k + 1]
-        inverse_pivots = jnp.where(row_id == k, inverse, inverse_pivots)
-        if k + 1 < rank:
-            multiplier = jnp.where(row_id > k, state[:, k : k + 1] * inverse, 0.0)
-            state = state - multiplier * row
+    inverse_pivots = jnp.zeros((rank, 2 * rank), F32)
+    for k in range(0, rank, w):
+        rows = [state[k + j : k + j + 1, :] for j in range(w)]
+        cols = [jnp.broadcast_to(state[:, k + j : k + j + 1], state.shape) for j in range(w)]
+        block = {(i, j): cols[j][k + i : k + i + 1, :] for i in range(w) for j in range(i + 1)}
+        change = None
+        inverse, ratio = [], {}
+        for j in range(w):
+            inverse.append(1.0 / block[j, j])
+            for i in range(j + 1, w):
+                ratio[i, j] = block[i, j] * inverse[j]
+            for i in range(j + 1, w):
+                for l in range(j + 1, i + 1):
+                    block[i, l] = block[i, l] - ratio[i, j] * block[l, j]
+        for j in range(w):
+            for i in range(j + 1, w):
+                rows[i] = rows[i] - ratio[i, j] * rows[j]
+                cols[i] = cols[i] - ratio[i, j] * cols[j]
+            inverse_pivots = jnp.where(row_id == k + j, inverse[j], inverse_pivots)
+            if k + j + 1 < rank:
+                term = jnp.where(row_id > k + j, cols[j] * inverse[j], 0.0) * rows[j]
+                change = term if change is None else change + term
+        if change is not None:
+            state = state - change
     unit = state[:, rank:]
-    basis = exact(unit, p, (((1,), (0,)), ((), ()))) * inverse_pivots
-    out_ref[...] = exact(unit, basis, (((0,), (0,)), ((), ())))
+    basis = exact(unit, p, (((1,), (0,)), ((), ()))) * inverse_pivots[:, :1]
+    high, low = halves(exact(unit, basis, (((0,), (0,)), ((), ()))))
+    out_ref[...] = jnp.concatenate([high, high, low], axis=0).T
 
 
 def solve(projected):
     return pl.pallas_call(
-        solve_kernel,
-        out_shape=jax.ShapeDtypeStruct(projected.shape, F32),
+        functools.partial(solve_kernel, 8),
+        out_shape=jax.ShapeDtypeStruct((projected.shape[1], 3 * projected.shape[0]), BF16),
         compiler_params=params(4),
         name="solve",
     )(projected)
@@ -217,6 +235,11 @@
     return lax.ppermute(x, axis, [(i, (i + step) % size) for i in range(size)])
 
 
+def mirror(x, size):
+    pairs = [(i, size - 1 - i) for i in range(size)]
+    return lax.ppermute(x, ("yh", "yl"), pairs)
+
+
 def spread(x, axes, size):
     return lax.all_to_all(jnp.broadcast_to(x[None], (size,) + x.shape), axes, 0, 0)
 
@@ -226,31 +249,32 @@
 
 
 def local(sizes, gradient, feedback, warm_basis):
-    y, z, x = sizes["y"], sizes["z"], sizes["x"]
+    z, x = sizes["z"], sizes["x"]
+    y = sizes["yh"] * sizes["yl"]
     rank, cols = warm_basis.shape
     width = cols // y
     merged, mine, other = project(gradient[0], feedback[0], warm_basis)
 
     mine = mine + rotate(other, "core", 2, 1)
     mine = added(spread(mine, "z", z))
-    mine = added(spread(mine, ("y", "x"), y * x))
+    mine = added(spread(mine, ("yh", "yl", "x"), y * x))
     projected = jnp.concatenate([mine, rotate(mine, "core", 2, 1)])
 
     factor = partial_factor(projected, merged, y, (y * z, rank // z, width))
-    summed = added(lax.all_to_all(factor, ("y", "z"), 0, 0))
-    whole = spread(summed, "z", z)
-    arrived = [rotate(whole, "y", y, y - k) for k in range(1, y)]
+    summed = added(lax.all_to_all(factor, ("yh", "yl", "z"), 0, 0))
+    here = spread(summed, ("yl", "z"), y // 2 * z)
+    there = mirror(here, y)
     basis = solve(projected)
-    build = functools.partial(rebuild, basis, merged, count=y, replicas=y * z)
-    outs = build([whole], (0,))
-    approx, updated = build(arrived, (1, 2, 3), earlier=outs)
+    build = functools.partial(rebuild, basis, merged, replicas=y * z)
+    outs = build(here, False)
+    approx, updated = build(there, True, earlier=outs)
     return (approx, updated[None])
 
 
 def solution(mesh):
-    sizes = {"y": 4, "z": 8, "x": 4, "core": 2}
+    sizes = {"yh": 2, "yl": 2, "z": 8, "x": 4, "core": 2}
     inner = Mesh(mesh.devices.reshape(tuple(sizes.values())), tuple(sizes))
-    dp, mp = ("y", "z"), ("x", "core")
+    dp, mp = ("yh", "yl", "z"), ("x", "core")
     return jax.shard_map(
         functools.partial(local, sizes),
         mesh=inner,

time: 83.4 us -> 82.7 us (level); the launches traced: 83.2 us -> 81.6 us
  starting transfers between devices: 4.23 us -> 1.85 us
  waiting for transfers between devices: 2.35 us -> 4.72 us
  Pallas kernels: 11.4 us -> 9.23 us
    ppermute x5 -> x2, starting transfers between devices: 4.23 us -> 0.19 us  [rotate(): return lax.ppermute(x, axis, [(i, (i + step) % size) for i in range(size)])]
    ppermute x0 -> x1, waiting for transfers between devices: none -> 2.38 us  [mirror(): return lax.ppermute(x, ('yh', 'yl'), pairs)]
    pallas_call x3, Pallas kernels: 7.14 us -> 5.02 us  [the longest x2 3.7 us: rebuild(): pl.pallas_call(functools.partial(rebuild_kernel, 1.0 / replicas, across,...]
    ppermute x0 -> x1, starting transfers between devices: none -> 1.67 us  [mirror(): return lax.ppermute(x, ('yh', 'yl'), pairs)]
    ppermute x5 -> x2, waiting for transfers between devices: 2.35 us -> 2.34 us  [rotate(): return lax.ppermute(x, axis, [(i, (i + step) % size) for i in range(size)])]
  transfers between devices with their start and end apart: 5 -> 3, of which waited for: 2 -> 3; matrix products, arithmetic and copies ran while one was open for 0% -> 0% of each run, Pallas kernels for 6% -> 4%
where the time goes in v4:
time: 82.7 us; the launch traced here: 81.6 us
  blocking collectives  64.9 us (78%)
  Pallas kernels  9.23 us (11%)
  waiting for transfers between devices  4.72 us (6%)
  starting transfers between devices  1.85 us (2%)
    all_to_all x3, blocking collectives, spread(): lax.all_to_all(jnp.broadcast_to(x[None], (size,) + x.shape), axes, 0, 0)  45.9 us
    all_to_all x1, blocking collectives, local(): summed = added(lax.all_to_all(factor, ('yh', 'yl', 'z'), 0, 0))  19.1 us
    pallas_call x2, Pallas kernels, rebuild(): pl.pallas_call(functools.partial(rebuild_kernel, 1.0 / replicas, across,...  3.7 us
    pallas_call x1, Pallas kernels, project(): pl.pallas_call(functools.partial(project_kernel, cuts, inner), in_specs=[...  3.5 us
    ppermute x1, waiting for transfers between devices, mirror(): return lax.ppermute(x, ('yh', 'yl'), pairs)  2.38 us
    ppermute x2, waiting for transfers between devices, rotate(): return lax.ppermute(x, axis, [(i, (i + step) % size) for i in range(size)])  2.34 us
    ppermute x1, starting transfers between devices, mirror(): return lax.ppermute(x, ('yh', 'yl'), pairs)  1.67 us
  transfers between devices with their start and end apart: 3, of which 3 were waited for; matrix products, arithmetic and copies ran while one was open for 0% of the time, Pallas kernels for 4%

profile of v4, /device:TPU:2, one launch (start us, length us, event | category | flops | bytes accessed | tf_op | source)
XLA Modules:
  0.0 81.6 jit_solution(14195366226769075079)
XLA Ops:
  0.6 3.5 %project.1 = (f32[256,3584]{1,0:T(8,128)S(1)}, f32[16,256]{1,0:T(8,128)S(1)}, f32[16,256]{1,0:T(8,128)S(1)}) custom-call(bf16[256,3584]{1,0:T(8,128)(2,1)} %bitcast.11, f32[256,3584]{1,0:T(8,128)} %bitcast.10, f32[32,3584]{1,0:T(8,128)} %basis.1), custom_call_target="tpu_custom_call" | custom-call | tf_op jit(solution)/shard_map/project/pallas_call | solution.py:88
  4.1 0.1 collective-permute-start
  4.2 1.2 %collective-permute-done = f32[16,256]{1,0:T(8,128)S(1)} collective-permute-done((f32[16,256]{1,0:T(8,128)S(1)}, f32[16,256]{1,0:T(8,128)S(1)}, u32[]{:S(2)}, u32[]{:S(2)}) %collective-permute-start) | collective-permute-done | bytes 16416 | tf_op jit(solution)/shard_map/ppermute | solution.py:235
  5.4 17.7 %all_to_all.20 = f32[8,16,256]{2,1,0:T(8,128)S(1)} all-to-all(f32[8,16,256]{2,1,0:T(8,128)S(1)} %broadcast_in_dim.12), channel_id=1, replica_groups=mesh['yh'=2,'yl'=2,'z'=8,'x'=4,'core'=2] {'z'}, dimensions={0} | all-to-all | bytes 262144 | tf_op jit(solution)/shard_map/all_to_all | solution.py:244
  23.1 14.6 %all_to_all.21 = f32[16,16,256]{2,1,0:T(8,128)S(1)} all-to-all(f32[16,16,256]{2,1,0:T(8,128)S(1)} %broadcast_in_dim.27), channel_id=1, replica_groups=mesh['yh'=2,'yl'=2,'z'=8,'x'=4,'core'=2] {'yh','yl','x'}, dimensions={0} | all-to-all | bytes 524288 | tf_op jit(solution)/shard_map/all_to_all | solution.py:244
  37.8 0.1 collective-permute-start.1
  37.9 1.2 %collective-permute-done.1 = f32[16,256]{1,0:T(8,128)S(1)} collective-permute-done((f32[16,256]{1,0:T(8,128)S(1)}, f32[16,256]{1,0:T(8,128)S(1)}, u32[]{:S(2)}, u32[]{:S(2)}) %collective-permute-start.1) | collective-permute-done | bytes 16416 | tf_op jit(solution)/shard_map/ppermute | solution.py:235
  39.0 0.7 partial_factor.1
  39.8 19.1 %all_to_all.22 = f32[32,4,896]{2,1,0:T(4,128)S(1)} all-to-all(f32[32,4,896]{2,1,0:T(4,128)S(1)} %partial_factor.1), channel_id=1, replica_groups=mesh['yh'=2,'yl'=2,'z'=8,'x'=4,'core'=2] {'yh','yl','z'}, dimensions={0} | all-to-all | bytes 917504 | tf_op jit(solution)/shard_map/all_to_all | solution.py:264
  58.8 0.1 fusion.2
  58.9 13.6 %all_to_all.23.factor = f32[16,4,896]{2,1,0:T(4,128)S(1)} all-to-all(f32[16,4,896]{2,1,0:T(4,128)S(1)} %broadcast_in_dim.29), channel_id=1, replica_groups=mesh['yh'=2,'yl'=2,'z'=8,'x'=4,'core'=2] {'yl','z'}, dimensions={0} | all-to-all | bytes 458752 | tf_op jit(solution)/shard_map/all_to_all | solution.py:244
  72.5 1.7 %collective-permute-start.2 = (f32[16,4,896]{2,1,0:T(4,128)S(1)}, f32[16,4,896]{2,1,0:T(4,128)S(1)}, u32[]{:S(2)}, u32[]{:S(2)}) collective-permute-start(f32[16,4,896]{2,1,0:T(4,128)S(1)} %all_to_all.23.factor), channel_id=1, source_target_pairs={{0,192},{64,128},{128,64},{192,0},{1,193},{65,129},{129,65},{193,1... | collective-permute-start | bytes 688136 | tf_op jit(solution)/shard_map/ppermute | solution.py:240
  74.2 1.3 %solve.1.basis = bf16[256,96]{1,0:T(8,128)(2,1)S(1)} custom-call(f32[32,256]{1,0:T(8,128)S(1)} %pad_maximum_fusion.projected_ref.projected), custom_call_target="tpu_custom_call" | custom-call | tf_op jit(solution)/shard_map/solve/pallas_call | solution.py:226
  75.5 1.8 %rebuild.2 = (bf16[256,3584]{1,0:T(8,128)(2,1)}, f32[256,3584]{1,0:T(8,128)}) custom-call(bf16[256,96]{1,0:T(8,128)(2,1)S(1)} %solve.1.basis, f32[256,3584]{1,0:T(8,128)S(1)} %get-tuple-element.11.merged, f32[16,4,896]{2,1,0:T(4,128)S(1)} %all_to_all.23.factor), custom_call_target="tpu_custom_call" | custom-call | tf_op jit(solution)/shard_map/rebuild/pallas_call | solution.py:165
  77.4 2.4 %collective-permute-done.2.factor = f32[16,4,896]{2,1,0:T(4,128)S(1)} collective-permute-done((f32[16,4,896]{2,1,0:T(4,128)S(1)}, f32[16,4,896]{2,1,0:T(4,128)S(1)}, u32[]{:S(2)}, u32[]{:S(2)}) %collective-permute-start.2) | collective-permute-done | bytes 229408 | tf_op jit(solution)/shard_map/ppermute | solution.py:240
  79.8 1.9 %rebuild.3 = (bf16[256,3584]{1,0:T(8,128)(2,1)}, f32[256,3584]{1,0:T(8,128)}) custom-call(bf16[256,96]{1,0:T(8,128)(2,1)S(1)} %solve.1.basis, f32[256,3584]{1,0:T(8,128)S(1)} %get-tuple-element.11.merged, f32[16,4,896]{2,1,0:T(4,128)S(1)} %collective-permute-done.2.factor, ...), custom_call_target="tpu_custom_call", output_to_operand_aliasing={{0}: (3, {}), {1}: (4, {})} | custom-call | tf_op jit(solution)/shard_map/rebuild/pallas_call | solution.py:165
  (7 shorter events, 0.1 us)
Async XLA Ops:
  4.1 1.3 %collective-permute-start = (f32[16,256]{1,0:T(8,128)S(1)}, f32[16,256]{1,0:T(8,128)S(1)}, u32[]{:S(2)}, u32[]{:S(2)}) collective-permute-start(f32[16,256]{1,0:T(8,128)S(1)} %get-tuple-element.10), channel_id=1, source_target_pairs={{0,1},{1,0},{2,3},{3,2},{4,5},{5,4},{6,7},{7,6},{8,9},{9,8},{10,11... | collective-permute-start | bytes 49160 | tf_op jit(solution)/shard_map/ppermute | solution.py:235
  37.8 1.3 %collective-permute-start.1 = (f32[16,256]{1,0:T(8,128)S(1)}, f32[16,256]{1,0:T(8,128)S(1)}, u32[]{:S(2)}, u32[]{:S(2)}) collective-permute-start(f32[16,256]{1,0:T(8,128)S(1)} %fusion), channel_id=1, source_target_pairs={{0,1},{1,0},{2,3},{3,2},{4,5},{5,4},{6,7},{7,6},{8,9},{9,8},{10,11... | collective-permute-start | bytes 49160 | tf_op jit(solution)/shard_map/ppermute | solution.py:235
  72.5 7.2 %collective-permute-start.2 = (f32[16,4,896]{2,1,0:T(4,128)S(1)}, f32[16,4,896]{2,1,0:T(4,128)S(1)}, u32[]{:S(2)}, u32[]{:S(2)}) collective-permute-start(f32[16,4,896]{2,1,0:T(4,128)S(1)} %all_to_all.23.factor), channel_id=1, source_target_pairs={{0,192},{64,128},{128,64},{192,0},{1,193},{65,129},{129,65},{193,1... | collective-permute-start | bytes 688136 | tf_op jit(solution)/shard_map/ppermute | solution.py:240

commit v5 on v4

--- a/solution.py
+++ b/solution.py
@@ -33,6 +33,10 @@
     for size in cuts:
         yield pl.ds(start, size)
         start += size
+
+
+def column_block_at(start, width):
+    return pl.ds(pl.multiple_of(start, 128), width)
 
 
 def column_block(index, width):
@@ -142,16 +146,17 @@
     for i in range(count):
         f = factor[i * groups : (i + 1) * groups].reshape(rank, width)
         f_high, f_low = halves(f)
-        value = dot(left, jnp.concatenate([f_high, f_low, f_high], axis=0), 1, 0)
-        part = column_block(2 * place + i, width)
-        a_buf[i] = value.astype(BF16)
-        u_buf[i] = merged[:, part] - value * scale
-        for copy in (
-            pltpu.make_async_copy(u_buf.at[i], updated.at[:, part], u_sem.at[i]),
-            pltpu.make_async_copy(a_buf.at[i], approx.at[:, part], a_sem.at[i]),
-        ):
-            copy.start()
-            copies.append(copy)
+        right = jnp.concatenate([f_high, f_low, f_high], axis=0)
+        start = (2 * place + i) * width
+        for j, (at, size) in enumerate(((0, 384), (384, 512))):
+            value = dot(left, right[:, at : at + size], 1, 0)
+            part = column_block_at(start + at, size)
+            a_buf[i, :, at : at + size] = value.astype(BF16)
+            u_buf[i, :, at : at + size] = merged[:, part] - value * scale
+            for buf, out, sem in ((u_buf, updated, u_sem), (a_buf, approx, a_sem)):
+                copy = pltpu.make_async_copy(buf.at[i, :, pl.ds(at, size)], out.at[:, part], sem.at[2 * i + j])
+                copy.start()
+                copies.append(copy)
     for copy in copies:
         copy.wait()
 
@@ -171,8 +176,8 @@
         scratch_shapes=[
             pltpu.VMEM((count, rows, width), BF16),
             pltpu.VMEM((count, rows, width), F32),
-            pltpu.SemaphoreType.DMA((count,)),
-            pltpu.SemaphoreType.DMA((count,)),
+            pltpu.SemaphoreType.DMA((2 * count,)),
+            pltpu.SemaphoreType.DMA((2 * count,)),
         ],
         compiler_params=params(20),
         name="rebuild",
@@ -256,8 +261,8 @@
     merged, mine, other = project(gradient[0], feedback[0], warm_basis)
 
     mine = mine + rotate(other, "core", 2, 1)
+    mine = added(spread(mine, ("yh", "yl", "x"), y * x))
     mine = added(spread(mine, "z", z))
-    mine = added(spread(mine, ("yh", "yl", "x"), y * x))
     projected = jnp.concatenate([mine, rotate(mine, "core", 2, 1)])
 
     factor = partial_factor(projected, merged, y, (y * z, rank // z, width))

time: 82.7 us -> 82.6 us (level)
  no operation moved by 1% of the time
where the time goes in v5:
time: 82.6 us; the launch traced here: 81.6 us
  blocking collectives  64.9 us (79%)
  Pallas kernels  9.17 us (11%)
  waiting for transfers between devices  4.75 us (6%)
  starting transfers between devices  1.85 us (2%)
    all_to_all x3, blocking collectives, spread(): lax.all_to_all(jnp.broadcast_to(x[None], (size,) + x.shape), axes, 0, 0)  45.9 us
    all_to_all x1, blocking collectives, local(): summed = added(lax.all_to_all(factor, ('yh', 'yl', 'z'), 0, 0))  19.1 us
    pallas_call x2, Pallas kernels, rebuild(): pl.pallas_call(functools.partial(rebuild_kernel, 1.0 / replicas, across,...  3.64 us
    pallas_call x1, Pallas kernels, project(): pl.pallas_call(functools.partial(project_kernel, cuts, inner), in_specs=[...  3.5 us
    ppermute x1, waiting for transfers between devices, mirror(): return lax.ppermute(x, ('yh', 'yl'), pairs)  2.41 us
    ppermute x2, waiting for transfers between devices, rotate(): return lax.ppermute(x, axis, [(i, (i + step) % size) for i in range(size)])  2.34 us
    ppermute x1, starting transfers between devices, mirror(): return lax.ppermute(x, ('yh', 'yl'), pairs)  1.67 us
  transfers between devices with their start and end apart: 3, of which 3 were waited for; matrix products, arithmetic and copies ran while one was open for 0% of the time, Pallas kernels for 4%

profile of v5, /device:TPU:2, one launch (start us, length us, event | category | flops | bytes accessed | tf_op | source)
XLA Modules:
  0.0 81.6 jit_solution(9943784042018596879)
XLA Ops:
  0.6 3.5 %project.1 = (f32[256,3584]{1,0:T(8,128)S(1)}, f32[16,256]{1,0:T(8,128)S(1)}, f32[16,256]{1,0:T(8,128)S(1)}) custom-call(bf16[256,3584]{1,0:T(8,128)(2,1)} %bitcast.11, f32[256,3584]{1,0:T(8,128)} %bitcast.10, f32[32,3584]{1,0:T(8,128)} %basis.1), custom_call_target="tpu_custom_call" | custom-call | tf_op jit(solution)/shard_map/project/pallas_call | solution.py:92
  4.1 0.1 collective-permute-start
  4.2 1.2 %collective-permute-done = f32[16,256]{1,0:T(8,128)S(1)} collective-permute-done((f32[16,256]{1,0:T(8,128)S(1)}, f32[16,256]{1,0:T(8,128)S(1)}, u32[]{:S(2)}, u32[]{:S(2)}) %collective-permute-start) | collective-permute-done | bytes 16416 | tf_op jit(solution)/shard_map/ppermute | solution.py:240
  5.4 14.9 %all_to_all.20 = f32[16,16,256]{2,1,0:T(8,128)S(1)} all-to-all(f32[16,16,256]{2,1,0:T(8,128)S(1)} %broadcast_in_dim.12), channel_id=1, replica_groups=mesh['yh'=2,'yl'=2,'z'=8,'x'=4,'core'=2] {'yh','yl','x'}, dimensions={0} | all-to-all | bytes 524288 | tf_op jit(solution)/shard_map/all_to_all | solution.py:249
  20.4 17.3 %all_to_all.21 = f32[8,16,256]{2,1,0:T(8,128)S(1)} all-to-all(f32[8,16,256]{2,1,0:T(8,128)S(1)} %broadcast_in_dim.27), channel_id=1, replica_groups=mesh['yh'=2,'yl'=2,'z'=8,'x'=4,'core'=2] {'z'}, dimensions={0} | all-to-all | bytes 262144 | tf_op jit(solution)/shard_map/all_to_all | solution.py:249
  37.8 0.1 collective-permute-start.1
  37.9 1.2 %collective-permute-done.1 = f32[16,256]{1,0:T(8,128)S(1)} collective-permute-done((f32[16,256]{1,0:T(8,128)S(1)}, f32[16,256]{1,0:T(8,128)S(1)}, u32[]{:S(2)}, u32[]{:S(2)}) %collective-permute-start.1) | collective-permute-done | bytes 16416 | tf_op jit(solution)/shard_map/ppermute | solution.py:240
  39.0 0.7 partial_factor.1
  39.8 19.1 %all_to_all.22 = f32[32,4,896]{2,1,0:T(4,128)S(1)} all-to-all(f32[32,4,896]{2,1,0:T(4,128)S(1)} %partial_factor.1), channel_id=1, replica_groups=mesh['yh'=2,'yl'=2,'z'=8,'x'=4,'core'=2] {'yh','yl','z'}, dimensions={0} | all-to-all | bytes 917504 | tf_op jit(solution)/shard_map/all_to_all | solution.py:269
  58.8 0.1 fusion.2
  58.9 13.6 %all_to_all.23.factor = f32[16,4,896]{2,1,0:T(4,128)S(1)} all-to-all(f32[16,4,896]{2,1,0:T(4,128)S(1)} %broadcast_in_dim.29), channel_id=1, replica_groups=mesh['yh'=2,'yl'=2,'z'=8,'x'=4,'core'=2] {'yl','z'}, dimensions={0} | all-to-all | bytes 458752 | tf_op jit(solution)/shard_map/all_to_all | solution.py:249
  72.5 1.7 %collective-permute-start.2 = (f32[16,4,896]{2,1,0:T(4,128)S(1)}, f32[16,4,896]{2,1,0:T(4,128)S(1)}, u32[]{:S(2)}, u32[]{:S(2)}) collective-permute-start(f32[16,4,896]{2,1,0:T(4,128)S(1)} %all_to_all.23.factor), channel_id=1, source_target_pairs={{0,192},{64,128},{128,64},{192,0},{1,193},{65,129},{129,65},{193,1... | collective-permute-start | bytes 688136 | tf_op jit(solution)/shard_map/ppermute | solution.py:245
  74.2 1.3 %solve.1.basis = bf16[256,96]{1,0:T(8,128)(2,1)S(1)} custom-call(f32[32,256]{1,0:T(8,128)S(1)} %pad_maximum_fusion.projected_ref.projected), custom_call_target="tpu_custom_call" | custom-call | tf_op jit(solution)/shard_map/solve/pallas_call | solution.py:231
  75.5 1.8 %rebuild.2 = (bf16[256,3584]{1,0:T(8,128)(2,1)}, f32[256,3584]{1,0:T(8,128)}) custom-call(bf16[256,96]{1,0:T(8,128)(2,1)S(1)} %solve.1.basis, f32[256,3584]{1,0:T(8,128)S(1)} %get-tuple-element.11.merged, f32[16,4,896]{2,1,0:T(4,128)S(1)} %all_to_all.23.factor), custom_call_target="tpu_custom_call" | custom-call | tf_op jit(solution)/shard_map/rebuild/pallas_call | solution.py:170
  77.4 2.4 %collective-permute-done.2.factor = f32[16,4,896]{2,1,0:T(4,128)S(1)} collective-permute-done((f32[16,4,896]{2,1,0:T(4,128)S(1)}, f32[16,4,896]{2,1,0:T(4,128)S(1)}, u32[]{:S(2)}, u32[]{:S(2)}) %collective-permute-start.2) | collective-permute-done | bytes 229408 | tf_op jit(solution)/shard_map/ppermute | solution.py:245
  79.8 1.8 %rebuild.3 = (bf16[256,3584]{1,0:T(8,128)(2,1)}, f32[256,3584]{1,0:T(8,128)}) custom-call(bf16[256,96]{1,0:T(8,128)(2,1)S(1)} %solve.1.basis, f32[256,3584]{1,0:T(8,128)S(1)} %get-tuple-element.11.merged, f32[16,4,896]{2,1,0:T(4,128)S(1)} %collective-permute-done.2.factor, ...), custom_call_target="tpu_custom_call", output_to_operand_aliasing={{0}: (3, {}), {1}: (4, {})} | custom-call | tf_op jit(solution)/shard_map/rebuild/pallas_call | solution.py:170
  (7 shorter events, 0.1 us)
Async XLA Ops:
  4.1 1.3 %collective-permute-start = (f32[16,256]{1,0:T(8,128)S(1)}, f32[16,256]{1,0:T(8,128)S(1)}, u32[]{:S(2)}, u32[]{:S(2)}) collective-permute-start(f32[16,256]{1,0:T(8,128)S(1)} %get-tuple-element.10), channel_id=1, source_target_pairs={{0,1},{1,0},{2,3},{3,2},{4,5},{5,4},{6,7},{7,6},{8,9},{9,8},{10,11... | collective-permute-start | bytes 49160 | tf_op jit(solution)/shard_map/ppermute | solution.py:240
  37.8 1.3 %collective-permute-start.1 = (f32[16,256]{1,0:T(8,128)S(1)}, f32[16,256]{1,0:T(8,128)S(1)}, u32[]{:S(2)}, u32[]{:S(2)}) collective-permute-start(f32[16,256]{1,0:T(8,128)S(1)} %fusion), channel_id=1, source_target_pairs={{0,1},{1,0},{2,3},{3,2},{4,5},{5,4},{6,7},{7,6},{8,9},{9,8},{10,11... | collective-permute-start | bytes 49160 | tf_op jit(solution)/shard_map/ppermute | solution.py:240
  72.5 7.2 %collective-permute-start.2 = (f32[16,4,896]{2,1,0:T(4,128)S(1)}, f32[16,4,896]{2,1,0:T(4,128)S(1)}, u32[]{:S(2)}, u32[]{:S(2)}) collective-permute-start(f32[16,4,896]{2,1,0:T(4,128)S(1)} %all_to_all.23.factor), channel_id=1, source_target_pairs={{0,192},{64,128},{128,64},{192,0},{1,193},{65,129},{129,65},{193,1... | collective-permute-start | bytes 688136 | tf_op jit(solution)/shard_map/ppermute | solution.py:245

commit v6 on v5

--- a/solution.py
+++ b/solution.py
@@ -61,7 +61,6 @@
     fetch_basis.wait()
     w_high, w_low = halves(b_buf[...])
     stack = jnp.concatenate([w_high, w_low], axis=0)
-    terms = []
     for i, part in enumerate(spans(cuts)):
         for copy in fetch[i]:
             copy.wait()
@@ -75,8 +74,7 @@
             term = both[:, :rank] + both[:, rank:]
             term = term + dot(low, w_high[:, at : at + inner], 1, 1)
             total = term if total is None else total + term
-        terms.append(total)
-    p_buf[...] = jnp.concatenate(terms, axis=0).T
+        p_buf[:, part] = total.T
     half = rank // 2
     mine[...] = p_buf[pl.ds(pl.multiple_of(core * half, 8), half)]
     other[...] = p_buf[pl.ds(pl.multiple_of((1 - core) * half, 8), half)]

time: 82.6 us -> 82.6 us (level)
  no operation moved by 1% of the time
where the time goes in v6:
time: 82.6 us; the launch traced here: 81.6 us
  blocking collectives  64.9 us (79%)
  Pallas kernels  9.17 us (11%)
  waiting for transfers between devices  4.75 us (6%)
  starting transfers between devices  1.85 us (2%)
    all_to_all x3, blocking collectives, spread(): lax.all_to_all(jnp.broadcast_to(x[None], (size,) + x.shape), axes, 0, 0)  45.9 us
    all_to_all x1, blocking collectives, local(): summed = added(lax.all_to_all(factor, ('yh', 'yl', 'z'), 0, 0))  19.1 us
    pallas_call x2, Pallas kernels, rebuild(): pl.pallas_call(functools.partial(rebuild_kernel, 1.0 / replicas, across,...  3.64 us
    pallas_call x1, Pallas kernels, project(): pl.pallas_call(functools.partial(project_kernel, cuts, inner), in_specs=[...  3.5 us
    ppermute x1, waiting for transfers between devices, mirror(): return lax.ppermute(x, ('yh', 'yl'), pairs)  2.41 us
    ppermute x2, waiting for transfers between devices, rotate(): return lax.ppermute(x, axis, [(i, (i + step) % size) for i in range(size)])  2.34 us
    ppermute x1, starting transfers between devices, mirror(): return lax.ppermute(x, ('yh', 'yl'), pairs)  1.67 us
  transfers between devices with their start and end apart: 3, of which 3 were waited for; matrix products, arithmetic and copies ran while one was open for 0% of the time, Pallas kernels for 4%

profile of v6, /device:TPU:2, one launch (start us, length us, event | category | flops | bytes accessed | tf_op | source)
XLA Modules:
  0.0 81.6 jit_solution(16652036291935055838)
XLA Ops:
  0.6 3.5 %project.1 = (f32[256,3584]{1,0:T(8,128)S(1)}, f32[16,256]{1,0:T(8,128)S(1)}, f32[16,256]{1,0:T(8,128)S(1)}) custom-call(bf16[256,3584]{1,0:T(8,128)(2,1)} %bitcast.11, f32[256,3584]{1,0:T(8,128)} %bitcast.10, f32[32,3584]{1,0:T(8,128)} %basis.1), custom_call_target="tpu_custom_call" | custom-call | tf_op jit(solution)/shard_map/project/pallas_call | solution.py:90
  4.1 0.1 collective-permute-start
  4.2 1.2 %collective-permute-done = f32[16,256]{1,0:T(8,128)S(1)} collective-permute-done((f32[16,256]{1,0:T(8,128)S(1)}, f32[16,256]{1,0:T(8,128)S(1)}, u32[]{:S(2)}, u32[]{:S(2)}) %collective-permute-start) | collective-permute-done | bytes 16416 | tf_op jit(solution)/shard_map/ppermute | solution.py:238
  5.4 14.9 %all_to_all.20 = f32[16,16,256]{2,1,0:T(8,128)S(1)} all-to-all(f32[16,16,256]{2,1,0:T(8,128)S(1)} %broadcast_in_dim.12), channel_id=1, replica_groups=mesh['yh'=2,'yl'=2,'z'=8,'x'=4,'core'=2] {'yh','yl','x'}, dimensions={0} | all-to-all | bytes 524288 | tf_op jit(solution)/shard_map/all_to_all | solution.py:247
  20.4 17.3 %all_to_all.21 = f32[8,16,256]{2,1,0:T(8,128)S(1)} all-to-all(f32[8,16,256]{2,1,0:T(8,128)S(1)} %broadcast_in_dim.27), channel_id=1, replica_groups=mesh['yh'=2,'yl'=2,'z'=8,'x'=4,'core'=2] {'z'}, dimensions={0} | all-to-all | bytes 262144 | tf_op jit(solution)/shard_map/all_to_all | solution.py:247
  37.8 0.1 collective-permute-start.1
  37.9 1.2 %collective-permute-done.1 = f32[16,256]{1,0:T(8,128)S(1)} collective-permute-done((f32[16,256]{1,0:T(8,128)S(1)}, f32[16,256]{1,0:T(8,128)S(1)}, u32[]{:S(2)}, u32[]{:S(2)}) %collective-permute-start.1) | collective-permute-done | bytes 16416 | tf_op jit(solution)/shard_map/ppermute | solution.py:238
  39.0 0.7 partial_factor.1
  39.8 19.1 %all_to_all.22 = f32[32,4,896]{2,1,0:T(4,128)S(1)} all-to-all(f32[32,4,896]{2,1,0:T(4,128)S(1)} %partial_factor.1), channel_id=1, replica_groups=mesh['yh'=2,'yl'=2,'z'=8,'x'=4,'core'=2] {'yh','yl','z'}, dimensions={0} | all-to-all | bytes 917504 | tf_op jit(solution)/shard_map/all_to_all | solution.py:267
  58.8 0.1 fusion.2
  58.9 13.6 %all_to_all.23.factor = f32[16,4,896]{2,1,0:T(4,128)S(1)} all-to-all(f32[16,4,896]{2,1,0:T(4,128)S(1)} %broadcast_in_dim.29), channel_id=1, replica_groups=mesh['yh'=2,'yl'=2,'z'=8,'x'=4,'core'=2] {'yl','z'}, dimensions={0} | all-to-all | bytes 458752 | tf_op jit(solution)/shard_map/all_to_all | solution.py:247
  72.5 1.7 %collective-permute-start.2 = (f32[16,4,896]{2,1,0:T(4,128)S(1)}, f32[16,4,896]{2,1,0:T(4,128)S(1)}, u32[]{:S(2)}, u32[]{:S(2)}) collective-permute-start(f32[16,4,896]{2,1,0:T(4,128)S(1)} %all_to_all.23.factor), channel_id=1, source_target_pairs={{0,192},{64,128},{128,64},{192,0},{1,193},{65,129},{129,65},{193,1... | collective-permute-start | bytes 688136 | tf_op jit(solution)/shard_map/ppermute | solution.py:243
  74.2 1.3 %solve.1.basis = bf16[256,96]{1,0:T(8,128)(2,1)S(1)} custom-call(f32[32,256]{1,0:T(8,128)S(1)} %pad_maximum_fusion.projected_ref.projected), custom_call_target="tpu_custom_call" | custom-call | tf_op jit(solution)/shard_map/solve/pallas_call | solution.py:229
  75.5 1.8 %rebuild.2 = (bf16[256,3584]{1,0:T(8,128)(2,1)}, f32[256,3584]{1,0:T(8,128)}) custom-call(bf16[256,96]{1,0:T(8,128)(2,1)S(1)} %solve.1.basis, f32[256,3584]{1,0:T(8,128)S(1)} %get-tuple-element.11.merged, f32[16,4,896]{2,1,0:T(4,128)S(1)} %all_to_all.23.factor), custom_call_target="tpu_custom_call" | custom-call | tf_op jit(solution)/shard_map/rebuild/pallas_call | solution.py:168
  77.4 2.4 %collective-permute-done.2.factor = f32[16,4,896]{2,1,0:T(4,128)S(1)} collective-permute-done((f32[16,4,896]{2,1,0:T(4,128)S(1)}, f32[16,4,896]{2,1,0:T(4,128)S(1)}, u32[]{:S(2)}, u32[]{:S(2)}) %collective-permute-start.2) | collective-permute-done | bytes 229408 | tf_op jit(solution)/shard_map/ppermute | solution.py:243
  79.8 1.8 %rebuild.3 = (bf16[256,3584]{1,0:T(8,128)(2,1)}, f32[256,3584]{1,0:T(8,128)}) custom-call(bf16[256,96]{1,0:T(8,128)(2,1)S(1)} %solve.1.basis, f32[256,3584]{1,0:T(8,128)S(1)} %get-tuple-element.11.merged, f32[16,4,896]{2,1,0:T(4,128)S(1)} %collective-permute-done.2.factor, ...), custom_call_target="tpu_custom_call", output_to_operand_aliasing={{0}: (3, {}), {1}: (4, {})} | custom-call | tf_op jit(solution)/shard_map/rebuild/pallas_call | solution.py:168
  (7 shorter events, 0.1 us)
Async XLA Ops:
  4.1 1.3 %collective-permute-start = (f32[16,256]{1,0:T(8,128)S(1)}, f32[16,256]{1,0:T(8,128)S(1)}, u32[]{:S(2)}, u32[]{:S(2)}) collective-permute-start(f32[16,256]{1,0:T(8,128)S(1)} %get-tuple-element.10), channel_id=1, source_target_pairs={{0,1},{1,0},{2,3},{3,2},{4,5},{5,4},{6,7},{7,6},{8,9},{9,8},{10,11... | collective-permute-start | bytes 49160 | tf_op jit(solution)/shard_map/ppermute | solution.py:238
  37.8 1.3 %collective-permute-start.1 = (f32[16,256]{1,0:T(8,128)S(1)}, f32[16,256]{1,0:T(8,128)S(1)}, u32[]{:S(2)}, u32[]{:S(2)}) collective-permute-start(f32[16,256]{1,0:T(8,128)S(1)} %fusion), channel_id=1, source_target_pairs={{0,1},{1,0},{2,3},{3,2},{4,5},{5,4},{6,7},{7,6},{8,9},{9,8},{10,11... | collective-permute-start | bytes 49160 | tf_op jit(solution)/shard_map/ppermute | solution.py:238
  72.5 7.2 %collective-permute-start.2 = (f32[16,4,896]{2,1,0:T(4,128)S(1)}, f32[16,4,896]{2,1,0:T(4,128)S(1)}, u32[]{:S(2)}, u32[]{:S(2)}) collective-permute-start(f32[16,4,896]{2,1,0:T(4,128)S(1)} %all_to_all.23.factor), channel_id=1, source_target_pairs={{0,192},{64,128},{128,64},{192,0},{1,193},{65,129},{129,65},{193,1... | collective-permute-start | bytes 688136 | tf_op jit(solution)/shard_map/ppermute | solution.py:243
